TPU v7x, 128 devices: a whole 4x4x4 slice. The times are simulated.
128 devices in a mesh: dp: 16 (over z_hi, x, core), seq: 8 (over y, z_lo).
Axes of the slice: x: 4, y: 4, z: 4 (z_hi: 2, z_lo: 2; z = z_hi * 2 + z_lo), core: 2. Of those that a mesh axis runs over, the one named last changes fastest.
Arguments:
- tokens: bfloat16 [1024, 16, 1024], P('seq', 'dp'), may hold values from -6 to 6
- cotangent: bfloat16 [1024, 16, 1024], P('seq', 'dp'), may hold values from -6 to 6
- lengths: int32 [16, 4], P('dp'), may hold values from 1 to 1021, as said below
- w_qkv: float32 [2, 1024, 3072], P(None, ('dp', 'seq')), may hold values from -0.1875 to 0.1875
- w_out: float32 [2, 1024, 1024], P(None, ('dp', 'seq')), may hold values from -0.1875 to 0.1875
- w_up: float32 [2, 1024, 4096], P(None, ('dp', 'seq')), may hold values from -0.1875 to 0.1875
- w_down: float32 [2, 4096, 1024], P(None, ('dp', 'seq')), may hold values from -0.09375 to 0.09375
- gains: float32 [2, 4, 1024], P(None, None, ('dp', 'seq')), may hold values from 0.5 to 1.5
- moment_qkv: float32 [2, 1024, 3072], P(None, ('dp', 'seq')), may hold values from -64 to 64
- moment_out: float32 [2, 1024, 1024], P(None, ('dp', 'seq')), may hold values from -64 to 64
- moment_up: float32 [2, 1024, 4096], P(None, ('dp', 'seq')), may hold values from -64 to 64
- moment_down: float32 [2, 4096, 1024], P(None, ('dp', 'seq')), may hold values from -64 to 64
- moment_gains: float32 [2, 4, 1024], P(None, None, ('dp', 'seq')), may hold values from -64 to 64
- square_qkv: float32 [2, 1024, 3072], P(None, ('dp', 'seq')), may hold values from 327.68 to 3276.8
- square_out: float32 [2, 1024, 1024], P(None, ('dp', 'seq')), may hold values from 327.68 to 3276.8
- square_up: float32 [2, 1024, 4096], P(None, ('dp', 'seq')), may hold values from 327.68 to 3276.8
- square_down: float32 [2, 4096, 1024], P(None, ('dp', 'seq')), may hold values from 327.68 to 3276.8
- square_gains: float32 [2, 4, 1024], P(None, None, ('dp', 'seq')), may hold values from 327.68 to 3276.8
Outputs:
- output: bfloat16 [1024, 16, 1024], P('seq', 'dp')
- input_grad: bfloat16 [1024, 16, 1024], P('seq', 'dp')
- new_qkv: float32 [2, 1024, 3072], P(None, ('dp', 'seq'))
- new_out: float32 [2, 1024, 1024], P(None, ('dp', 'seq'))
- new_up: float32 [2, 1024, 4096], P(None, ('dp', 'seq'))
- new_down: float32 [2, 4096, 1024], P(None, ('dp', 'seq'))
- new_gains: float32 [2, 4, 1024], P(None, None, ('dp', 'seq'))
- next_moment_qkv: float32 [2, 1024, 3072], P(None, ('dp', 'seq'))
- next_moment_out: float32 [2, 1024, 1024], P(None, ('dp', 'seq'))
- next_moment_up: float32 [2, 1024, 4096], P(None, ('dp', 'seq'))
- next_moment_down: float32 [2, 4096, 1024], P(None, ('dp', 'seq'))
- next_moment_gains: float32 [2, 4, 1024], P(None, None, ('dp', 'seq'))
- next_square_qkv: float32 [2, 1024, 3072], P(None, ('dp', 'seq'))
- next_square_out: float32 [2, 1024, 1024], P(None, ('dp', 'seq'))
- next_square_up: float32 [2, 1024, 4096], P(None, ('dp', 'seq'))
- next_square_down: float32 [2, 4096, 1024], P(None, ('dp', 'seq'))
- next_square_gains: float32 [2, 4, 1024], P(None, None, ('dp', 'seq'))
- copy_qkv: bfloat16 [2, 1024, 3072], P(None, ('dp', 'seq'))
- copy_out: bfloat16 [2, 1024, 1024], P(None, ('dp', 'seq'))
- copy_up: bfloat16 [2, 1024, 4096], P(None, ('dp', 'seq'))
- copy_down: bfloat16 [2, 4096, 1024], P(None, ('dp', 'seq'))
- copy_gains: bfloat16 [2, 4, 1024], P(None, None, ('dp', 'seq'))
Inputs may be any that keep to these rules, and one draw needn't show every extreme that they name: Each row's 4 document lengths are positive and sum to 1024.
All inputs are finite; a program needn't handle non-finite values.
Results may differ from a plain program's by a relative error of at most 0.025.
Values may be sent and summed in bfloat16 or wider, within the bound.
No kernel may reach another device: no remote copies, remote signals or barrier semaphores. Data moves between devices by JAX's collectives and lax.ppermute only.
A program may use at most 256 MiB of HBM per device.

v0:
```python
from functools import partial

import jax
import jax.numpy as jnp
from jax import lax
from jax.sharding import PartitionSpec as P

D = 1024
HEADS = 16
HEAD_DIM = 64
LAYERS = 2
STEP = 5


norm_eps = 1e-05
beta_first = 0.9
beta_second = 0.95
adam_eps = 1e-08
weight_decay = 0.1
rate_matrix = 0.04
rate_gain = 0.4
masked_score = -1e30


def rms_norm(values, gain_row):
    scaled = lax.rsqrt(jnp.mean(values * values, axis=-1, keepdims=True) + norm_eps)
    return values * scaled * gain_row


def rotate(values, cosine, sine_table):
    half_dim = values.shape[-1] // 2
    first_half = values[..., :half_dim]
    second_half = values[..., half_dim:]
    return jnp.concatenate(
        [
            first_half * cosine - second_half * sine_table,
            second_half * cosine + first_half * sine_table,
        ],
        axis=-1,
    )


def rotary_tables(positions):
    half_dim = HEAD_DIM // 2
    inverse = 10000.0 ** (-jnp.arange(half_dim, dtype=jnp.float32) / half_dim)
    angle = positions.astype(jnp.float32)[..., None] * inverse
    return (jnp.cos(angle), jnp.sin(angle))


def doc_tables(lengths, length_total):
    ends = jnp.cumsum(lengths, axis=-1)
    starts = ends - lengths
    places = jnp.arange(length_total, dtype=jnp.int32)
    doc_ids = jnp.sum((places[None, :, None] >= ends[:, None, :]).astype(jnp.int32), axis=-1)
    picked = doc_ids[:, :, None] == jnp.arange(lengths.shape[-1], dtype=jnp.int32)[None, None, :]
    first_place = jnp.sum(jnp.where(picked, starts[:, None, :], 0), axis=-1)
    return (doc_ids, places[None, :] - first_place)


def adam_update(master, moment_one, moment_two, gradient, rate, decay):
    moment_new = beta_first * moment_one + (1.0 - beta_first) * gradient
    square_new = beta_second * moment_two + (1.0 - beta_second) * gradient * gradient
    moment_hat = moment_new / (1.0 - beta_first**STEP)
    square_hat = square_new / (1.0 - beta_second**STEP)
    updated = master - rate * (moment_hat / (jnp.sqrt(square_hat) + adam_eps) + decay * master)
    return (updated, moment_new, square_new)


def attention_scores(queries, key_all, allowed, score_scale):
    raw_scores = (
        jnp.einsum("crhd,krhd->rhck", queries, key_all, preferred_element_type=jnp.float32)
        * score_scale
    )
    return jnp.where(allowed, raw_scores, masked_score)


def project(left, right):
    return jnp.einsum("crd,de->cre", left, right, preferred_element_type=jnp.float32)


def weight_grad(left, right):
    return jnp.einsum("crd,cre->de", left, right, preferred_element_type=jnp.float32)


def project_back(grad_rows, weight):
    return jnp.einsum("cre,de->crd", grad_rows, weight, preferred_element_type=jnp.float32)


def body(
    tokens,
    cotangent,
    lengths,
    w_qkv,
    w_out,
    w_up,
    w_down,
    gains,
    moment_qkv,
    moment_out,
    moment_up,
    moment_down,
    moment_gains,
    square_qkv,
    square_out,
    square_up,
    square_down,
    square_gains,
):
    block_rows = tokens.shape[0]
    row_count = tokens.shape[1]
    length_total = block_rows * lax.axis_size("seq")
    score_scale = HEAD_DIM ** (-0.5)
    weight_qkv, weight_out, weight_up, weight_down, gain_low = (
        lax.all_gather(w_qkv.astype(jnp.bfloat16), ("dp", "seq"), axis=1, tiled=True),
        lax.all_gather(w_out.astype(jnp.bfloat16), ("dp", "seq"), axis=1, tiled=True),
        lax.all_gather(w_up.astype(jnp.bfloat16), ("dp", "seq"), axis=1, tiled=True),
        lax.all_gather(w_down.astype(jnp.bfloat16), ("dp", "seq"), axis=1, tiled=True),
        lax.all_gather(gains.astype(jnp.bfloat16), ("dp", "seq"), axis=2, tiled=True),
    )
    gain_all = gain_low.astype(jnp.float32)
    doc_ids, positions = doc_tables(lengths, length_total)
    offset = lax.axis_index("seq") * block_rows
    local_docs = lax.dynamic_slice_in_dim(doc_ids, offset, block_rows, 1)
    local_positions = lax.dynamic_slice_in_dim(positions, offset, block_rows, 1)
    cosine, sine_table = rotary_tables(jnp.transpose(local_positions))
    cosine = cosine[:, :, None, :]
    sine_table = sine_table[:, :, None, :]
    places_all = jnp.arange(length_total, dtype=jnp.int32)
    places_local = offset + jnp.arange(block_rows, dtype=jnp.int32)
    allowed = (local_docs[:, :, None] == doc_ids[:, None, :]) & (
        places_all[None, None, :] <= places_local[None, :, None]
    )
    allowed = allowed[:, None]
    hidden = tokens.astype(jnp.float32)
    kept_state = []
    for layer_index in range(LAYERS):
        gain_rows = gain_all[layer_index]
        layer_input = hidden
        normed = rms_norm(hidden, gain_rows[0]).astype(jnp.bfloat16)
        mixed_qkv = project(normed, weight_qkv[layer_index])
        qkv_parts = mixed_qkv.reshape(block_rows, row_count, 3, HEADS, HEAD_DIM)
        queries = rotate(qkv_parts[:, :, 0], cosine, sine_table).astype(jnp.bfloat16)
        key_own = rotate(qkv_parts[:, :, 1], cosine, sine_table).astype(jnp.bfloat16)
        value_own = qkv_parts[:, :, 2].astype(jnp.bfloat16)
        key_all, value_all = (
            lax.all_gather(key_own, "seq", axis=0, tiled=True),
            lax.all_gather(value_own, "seq", axis=0, tiled=True),
        )
        scores = attention_scores(queries, key_all, allowed, score_scale)
        largest = jnp.max(scores, axis=-1, keepdims=True)
        exponent = jnp.exp(scores - largest)
        totals = jnp.sum(exponent, axis=-1, keepdims=True)
        probabilities = exponent / totals
        log_total = largest + jnp.log(totals)
        attended = jnp.einsum(
            "rhck,krhd->crhd",
            probabilities.astype(jnp.bfloat16),
            value_all,
            preferred_element_type=jnp.float32,
        )
        attended = attended.reshape(block_rows, row_count, D).astype(jnp.bfloat16)
        branch = project(attended, weight_out[layer_index])
        middle = hidden + rms_norm(branch, gain_rows[1])
        normed_mlp = rms_norm(middle, gain_rows[2]).astype(jnp.bfloat16)
        upward = project(normed_mlp, weight_up[layer_index])
        active = jax.nn.gelu(upward, approximate=False).astype(jnp.bfloat16)
        downward = project(active, weight_down[layer_index])
        hidden = middle + rms_norm(downward, gain_rows[3])
        stored_keys, stored_values = (key_all, value_all)
        kept_state.append(
            (
                layer_input,
                normed,
                queries,
                stored_keys,
                stored_values,
                log_total,
                attended,
                branch,
                middle,
                normed_mlp,
                upward,
                active,
                downward,
            )
        )
    output = hidden.astype(jnp.bfloat16)
    grad_hidden = cotangent.astype(jnp.float32)
    collected = []
    for layer_index in reversed(range(LAYERS)):
        (
            layer_input,
            normed,
            queries,
            stored_keys,
            stored_values,
            log_total,
            attended,
            branch,
            middle,
            normed_mlp,
            upward,
            active,
            downward,
        ) = kept_state[layer_index]
        gain_rows = gain_all[layer_index]
        _, norm_back = jax.vjp(rms_norm, downward, gain_rows[3])
        d_down, grad_three = norm_back(grad_hidden)
        d_down = d_down.astype(jnp.bfloat16)
        grad_wdown = weight_grad(active, d_down)
        d_active = project_back(d_down, weight_down[layer_index])
        _, gelu_back = jax.vjp(partial(jax.nn.gelu, approximate=False), upward)
        d_up = gelu_back(d_active)[0].astype(jnp.bfloat16)
        grad_wup = weight_grad(normed_mlp, d_up)
        d_normed = project_back(d_up, weight_up[layer_index])
        _, norm_back = jax.vjp(rms_norm, middle, gain_rows[2])
        d_middle, grad_two = norm_back(d_normed)
        d_middle = d_middle + grad_hidden
        _, norm_back = jax.vjp(rms_norm, branch, gain_rows[1])
        d_branch, grad_one = norm_back(d_middle)
        d_branch = d_branch.astype(jnp.bfloat16)
        grad_wout = weight_grad(attended, d_branch)
        d_att = project_back(d_branch, weight_out[layer_index]).astype(jnp.bfloat16)
        d_att = d_att.reshape(block_rows, row_count, HEADS, HEAD_DIM)
        key_all, value_all = (stored_keys, stored_values)
        scores = attention_scores(queries, key_all, allowed, score_scale)
        probabilities = jnp.exp(scores - log_total)
        d_prob = jnp.einsum("crhd,krhd->rhck", d_att, value_all, preferred_element_type=jnp.float32)
        row_delta = jnp.sum(probabilities * d_prob, axis=-1, keepdims=True)
        d_score = (probabilities * (d_prob - row_delta)).astype(jnp.bfloat16)
        d_query = (
            jnp.einsum("rhck,krhd->crhd", d_score, key_all, preferred_element_type=jnp.float32)
            * score_scale
        )
        probs_low = probabilities.astype(jnp.bfloat16)
        key_part = (
            jnp.einsum("rhck,crhd->krhd", d_score, queries, preferred_element_type=jnp.float32)
            * score_scale
        )
        value_part = jnp.einsum(
            "rhck,crhd->krhd", probs_low, d_att, preferred_element_type=jnp.float32
        )
        key_grads = lax.psum_scatter(
            jnp.stack([key_part, value_part], axis=2)
            .reshape(lax.axis_size("seq") * block_rows, row_count, 2 * D)
            .astype(jnp.bfloat16),
            "seq",
            scatter_dimension=0,
            tiled=True,
        ).astype(jnp.float32)
        key_grads = key_grads.reshape(block_rows, row_count, 2, HEADS, HEAD_DIM)
        d_mixed = jnp.stack(
            [
                rotate(d_query, cosine, -sine_table),
                rotate(key_grads[:, :, 0], cosine, -sine_table),
                key_grads[:, :, 1],
            ],
            axis=2,
        )
        d_mixed = d_mixed.reshape(block_rows, row_count, 3 * D).astype(jnp.bfloat16)
        grad_wqkv = weight_grad(normed, d_mixed)
        d_normed = project_back(d_mixed, weight_qkv[layer_index])
        _, norm_back = jax.vjp(rms_norm, layer_input, gain_rows[0])
        d_input, grad_zero = norm_back(d_normed)
        grad_hidden = d_input + d_middle
        layer_terms = (
            grad_wqkv,
            grad_wout,
            grad_wup,
            grad_wdown,
            jnp.stack([grad_zero, grad_one, grad_two, grad_three]),
        )
        collected.insert(0, layer_terms)
    input_grad = grad_hidden.astype(jnp.bfloat16)
    summed = tuple((jnp.stack([member[column] for member in collected]) for column in range(5)))
    summed = (
        lax.psum_scatter(summed[0], ("dp", "seq"), scatter_dimension=1, tiled=True),
        lax.psum_scatter(summed[1], ("dp", "seq"), scatter_dimension=1, tiled=True),
        lax.psum_scatter(summed[2], ("dp", "seq"), scatter_dimension=1, tiled=True),
        lax.psum_scatter(summed[3], ("dp", "seq"), scatter_dimension=1, tiled=True),
        lax.psum_scatter(summed[4], ("dp", "seq"), scatter_dimension=2, tiled=True),
    )
    upd_qkv = adam_update(w_qkv, moment_qkv, square_qkv, summed[0], rate_matrix, weight_decay)
    upd_out = adam_update(w_out, moment_out, square_out, summed[1], rate_matrix, weight_decay)
    upd_up = adam_update(w_up, moment_up, square_up, summed[2], rate_matrix, weight_decay)
    upd_down = adam_update(w_down, moment_down, square_down, summed[3], rate_matrix, weight_decay)
    upd_gains = adam_update(gains, moment_gains, square_gains, summed[4], rate_gain, 0.0)
    return (
        output,
        input_grad,
        upd_qkv[0],
        upd_out[0],
        upd_up[0],
        upd_down[0],
        upd_gains[0],
        upd_qkv[1],
        upd_out[1],
        upd_up[1],
        upd_down[1],
        upd_gains[1],
        upd_qkv[2],
        upd_out[2],
        upd_up[2],
        upd_down[2],
        upd_gains[2],
        upd_qkv[0].astype(jnp.bfloat16),
        upd_out[0].astype(jnp.bfloat16),
        upd_up[0].astype(jnp.bfloat16),
        upd_down[0].astype(jnp.bfloat16),
        upd_gains[0].astype(jnp.bfloat16),
    )


def solution(mesh):
    placed = (
        P("seq", "dp", None),
        P("seq", "dp", None),
        P("dp", None),
        P(None, ("dp", "seq"), None),
        P(None, ("dp", "seq"), None),
        P(None, ("dp", "seq"), None),
        P(None, ("dp", "seq"), None),
        P(None, None, ("dp", "seq")),
        P(None, ("dp", "seq"), None),
        P(None, ("dp", "seq"), None),
        P(None, ("dp", "seq"), None),
        P(None, ("dp", "seq"), None),
        P(None, None, ("dp", "seq")),
        P(None, ("dp", "seq"), None),
        P(None, ("dp", "seq"), None),
        P(None, ("dp", "seq"), None),
        P(None, ("dp", "seq"), None),
        P(None, None, ("dp", "seq")),
    )
    return jax.shard_map(
        body,
        mesh=mesh,
        in_specs=placed,
        out_specs=(
            P("seq", "dp", None),
            P("seq", "dp", None),
            P(None, ("dp", "seq"), None),
            P(None, ("dp", "seq"), None),
            P(None, ("dp", "seq"), None),
            P(None, ("dp", "seq"), None),
            P(None, None, ("dp", "seq")),
            P(None, ("dp", "seq"), None),
            P(None, ("dp", "seq"), None),
            P(None, ("dp", "seq"), None),
            P(None, ("dp", "seq"), None),
            P(None, None, ("dp", "seq")),
            P(None, ("dp", "seq"), None),
            P(None, ("dp", "seq"), None),
            P(None, ("dp", "seq"), None),
            P(None, ("dp", "seq"), None),
            P(None, None, ("dp", "seq")),
            P(None, ("dp", "seq"), None),
            P(None, ("dp", "seq"), None),
            P(None, ("dp", "seq"), None),
            P(None, ("dp", "seq"), None),
            P(None, None, ("dp", "seq")),
        ),
        check_vma=False,
    )
```

profile of v0, /device:TPU:1, one launch (start us, length us, event | category | flops | bytes accessed | tf_op | source)
XLA Modules:
  0.0 4694.3 jit_solution(13284051364844496279)
XLA Ops:
  9.7 305.8 %all_gather.27 = bf16[2,4,1024]{1,0,2:T(2,128)(2,1)S(1)} all-gather(bf16[2,4,8]{1,0,2:T(2,128)(2,1)S(1)} %copy.65), channel_id=1, replica_groups=mesh['dp'=16,'seq'=8] {'dp','seq'}, dimensions={2}, use_global_device_ids=true | all-gather | bytes 16512 | tf_op jit(solution)/shard_map/all_gather | solution.py:118
  317.2 27.1 slice_reduce_fusion
  344.5 10.5 slice_bitcast_fusion.12
  355.0 8.7 copy.66
  363.7 4.7 convolution_bitcast_fusion.9
  373.0 8.6 copy.67
  381.6 53.7 %all-gather.13.cloned.1.call-done = bf16[1024,1,16,64]{0,3,2,1:T(8,128)(2,1)} async-done(((bf16[128,1,16,64]{0,3,2,1:T(8,128)(2,1)}), bf16[1024,1,16,64]{0,3,2,1:T(8,128)(2,1)}) %all-gather.13.cloned.1.call-update) | async-done | bytes 2097168 | tf_op jit(solution)/shard_map/all_gather | solution.py:146
  438.6 3.3 copy-done
  443.7 53.2 %all-gather.23.cloned.1.call-done = bf16[1024,1,1,16,64]{0,4,3,2,1:T(8,128)(2,1)} async-done(((bf16[128,1,1,16,64]{0,4,3,2,1:T(8,128)(2,1)}), bf16[1024,1,1,16,64]{0,4,3,2,1:T(8,128)(2,1)}) %all-gather.23.cloned.1.call-update) | async-done | bytes 2097168 | tf_op jit(solution)/shard_map/all_gather | solution.py:147
  496.9 5.8 fusion.75
  502.8 306.2 %all-gather.15.cloned.1.call-done = bf16[2,1024,1024]{2,1,0:T(8,128)(2,1)} async-done(((bf16[2,8,1024]{2,1,0:T(8,128)(2,1)}), bf16[2,1024,1024]{2,1,0:T(8,128)(2,1)}) %all-gather.15.cloned.1.call-update) | async-done | bytes 4194320 | tf_op jit(solution)/shard_map/all_gather | solution.py:115
  812.2 326.8 %all-gather.17.cloned.1.call-done = bf16[2,1024,4096]{2,1,0:T(8,128)(2,1)} async-done(((bf16[2,8,4096]{2,1,0:T(8,128)(2,1)}), bf16[2,1024,4096]{2,1,0:T(8,128)(2,1)}) %all-gather.17.cloned.1.call-update) | async-done | bytes 16777232 | tf_op jit(solution)/shard_map/all_gather | solution.py:116
  1139.0 6.1 fusion.3
  1145.1 323.6 %all-gather.19.cloned.1.call-done = bf16[2,4096,1024]{2,1,0:T(8,128)(2,1)} async-done(((bf16[2,32,1024]{2,1,0:T(8,128)(2,1)}), bf16[2,4096,1024]{2,1,0:T(8,128)(2,1)}) %all-gather.19.cloned.1.call-update) | async-done | bytes 16777232 | tf_op jit(solution)/shard_map/all_gather | solution.py:117
  1468.7 8.2 multiply_reduce_fusion.6
  1477.2 4.7 convolution_bitcast_fusion.8
  1483.9 56.0 %all-gather.21.cloned.1.call-done = bf16[1024,1,16,64]{0,3,2,1:T(8,128)(2,1)} async-done(((bf16[128,1,16,64]{0,3,2,1:T(8,128)(2,1)}), bf16[1024,1,16,64]{0,3,2,1:T(8,128)(2,1)}) %all-gather.21.cloned.1.call-update) | async-done | bytes 2097168 | tf_op jit(solution)/shard_map/all_gather | solution.py:146
  1546.4 55.1 %all-gather.25.cloned.1.call-done = bf16[1024,1,1,16,64]{0,4,3,2,1:T(8,128)(2,1)} async-done(((bf16[128,1,1,16,64]{0,4,3,2,1:T(8,128)(2,1)}), bf16[1024,1,1,16,64]{0,4,3,2,1:T(8,128)(2,1)}) %all-gather.25.cloned.1.call-update) | async-done | bytes 2097168 | tf_op jit(solution)/shard_map/all_gather | solution.py:147
  1601.5 6.0 fusion.72
  1608.3 4.9 fusion.7
  1613.2 9.5 multiply_reduce_fusion.2
  1625.2 9.9 add_convert_fusion.1
  1635.1 3.5 fusion.98
  1642.3 5.2 convert_bitcast_fusion.1
  1647.5 4.9 multiply_reduce_fusion.1
  1658.6 6.5 copy.78
  1666.8 4.5 fusion.69
  1671.3 87.2 %reduce-scatter.20.cloned.1.call-done = bf16[128,2048]{1,0:T(8,128)(2,1)} async-done(((bf16[1024,2048]{1,0:T(8,128)(2,1)}), bf16[128,2048]{1,0:T(8,128)(2,1)}) %reduce-scatter.20.cloned.1.call-update) | async-done | bytes 524304
  1760.2 6.0 fusion.100
  1768.1 9.7 add_convert_fusion
  1777.9 3.5 fusion.102
  1784.4 5.2 convert_bitcast_fusion
  1789.6 4.9 multiply_reduce_fusion
  1800.7 6.5 copy.80
  1809.6 4.1 pad_maximum_fusion.3
  1813.8 7.8 convolution_bitcast_fusion.4
  1823.9 74.7 %reduce-scatter.22.cloned.1.call-done = bf16[128,2048]{1,0:T(8,128)(2,1)} async-done(((bf16[1024,2048]{1,0:T(8,128)(2,1)}), bf16[128,2048]{1,0:T(8,128)(2,1)}) %reduce-scatter.22.cloned.1.call-update) | async-done | bytes 524304
  1905.6 8.8 pad_maximum_fusion.2
  1915.3 7.9 convolution_bitcast_fusion
  1923.2 8.0 convolution_bitcast_fusion.1
  1931.2 11.4 pad_maximum_fusion.1
  1949.0 11.8 pad_maximum_fusion
  1961.7 5.2 fusion.85
  1967.0 66.9 %all-reduce = f32[2,4,1024]{2,1,0:T(4,128)S(1)} all-reduce(f32[2,4,1024]{2,1,0:T(4,128)S(1)} %pad_maximum_fusion.16), channel_id=10, replica_groups=mesh['dp'=16,'seq'=8] {'dp','seq'}, use_global_device_ids=true, to_apply=%region_39.40.clone | all-reduce | flops 8192 | bytes 65536
  2035.5 501.6 %reduce-scatter.14.cloned.1.call-done = f32[2,8,1024]{2,1,0:T(8,128)} async-done(((f32[2,1024,1024]{2,1,0:T(8,128)}), f32[2,8,1024]{2,1,0:T(8,128)}) %reduce-scatter.14.cloned.1.call-update) | async-done | bytes 65552 | tf_op jit(solution)/shard_map/reduce_scatter | solution.py:278
  2538.7 683.1 %reduce-scatter.12.cloned.1.call-done = f32[2,8,3072]{2,1,0:T(8,128)} async-done(((f32[2,1024,3072]{2,1,0:T(8,128)}), f32[2,8,3072]{2,1,0:T(8,128)}) %reduce-scatter.12.cloned.1.call-update) | async-done | bytes 196624 | tf_op jit(solution)/shard_map/reduce_scatter | solution.py:277
  3223.7 733.1 %reduce-scatter.18.cloned.1.call-done = f32[2,32,1024]{2,1,0:T(8,128)} async-done(((f32[2,4096,1024]{2,1,0:T(8,128)}), f32[2,32,1024]{2,1,0:T(8,128)}) %reduce-scatter.18.cloned.1.call-update) | async-done | bytes 262160 | tf_op jit(solution)/shard_map/reduce_scatter | solution.py:280
  3958.8 726.5 %reduce-scatter.16.cloned.1.call-done = f32[2,8,4096]{2,1,0:T(8,128)} async-done(((f32[2,1024,4096]{2,1,0:T(8,128)}), f32[2,8,4096]{2,1,0:T(8,128)}) %reduce-scatter.16.cloned.1.call-update) | async-done | bytes 262160 | tf_op jit(solution)/shard_map/reduce_scatter | solution.py:279
  (343 shorter events, 81.5 us)
Async XLA Ops:
  7.2 308.7 %copy-start.92 = (s32[1,4]{1,0:T(1,128)S(1)}, s32[1,4]{1,0:T(1,128)}, u32[]{:S(2)}) copy-start(s32[1,4]{1,0:T(1,128)} %param.20) | copy-start | bytes 52
  7.2 309.1 %copy-start.12 = (bf16[128,1,1024]{2,0,1:T(8,128)(2,1)S(1)}, bf16[128,1,1024]{2,0,1:T(8,128)(2,1)}, u32[]{:S(2)}) copy-start(bf16[128,1,1024]{2,0,1:T(8,128)(2,1)} %param.18) | copy-start | bytes 786436
  7.2 337.3 %all-gather.11.cloned.1.call-start = ((), (), s32[]{:S(2)}) async-start(), calls=%async_computation.6 | async-start | bytes 12681216 | tf_op jit(solution)/shard_map/all_gather | solution.py:114
  8.9 426.4 %all-gather.13.cloned.1.call-start = ((), (), s32[]{:S(2)}) async-start(), calls=%async_computation.7 | async-start | bytes 2359296 | tf_op jit(solution)/shard_map/all_gather | solution.py:146
  316.5 47.2 %copy-start.73 = (f32[128]{0:T(128)}, f32[128]{0:T(128)S(1)}, u32[]{:S(2)}) copy-start(f32[128]{0:T(128)S(1)} %fusion.138) | copy-start | bytes 1540
  344.4 466.7 %copy-start.66 = (f32[1024]{0:T(1024)}, f32[1024]{0:T(1024)S(1)}, u32[]{:S(2)}) copy-start(f32[1024]{0:T(1024)S(1)} %get-tuple-element.40) | copy-start | bytes 12292
  344.4 794.5 %copy-start.60 = (f32[1024]{0:T(1024)}, f32[1024]{0:T(1024)S(1)}, u32[]{:S(2)}) copy-start(f32[1024]{0:T(1024)S(1)} %get-tuple-element.39) | copy-start | bytes 12292
  344.4 1294.2 %copy-start.62 = (f32[1024]{0:T(1024)}, f32[1024]{0:T(1024)S(1)}, u32[]{:S(2)}) copy-start(f32[1024]{0:T(1024)S(1)} %get-tuple-element.35) | copy-start | bytes 12292
  368.6 66.7 %copy-start.28 = (bf16[128,16,32]{0,2,1:T(8,128)(2,1)}, bf16[128,16,32]{0,2,1:T(8,128)(2,1)S(1)}, u32[]{:S(2)}) copy-start(bf16[128,16,32]{0,2,1:T(8,128)(2,1)S(1)} %get-tuple-element.93) | copy-start | bytes 393220
  368.6 66.7 %copy-start.30 = (bf16[128,16,32]{0,2,1:T(8,128)(2,1)}, bf16[128,16,32]{0,2,1:T(8,128)(2,1)S(1)}, u32[]{:S(2)}) copy-start(bf16[128,16,32]{0,2,1:T(8,128)(2,1)S(1)} %get-tuple-element.94) | copy-start | bytes 393220
  369.4 127.5 %all-gather.23.cloned.1.call-start = ((), (), s32[]{:S(2)}) async-start(), calls=%async_computation.16 | async-start | bytes 2359296 | tf_op jit(solution)/shard_map/all_gather | solution.py:147
  370.2 438.7 %all-gather.15.cloned.1.call-start = ((), (), s32[]{:S(2)}) async-start(), calls=%async_computation.8 | async-start | bytes 4227072 | tf_op jit(solution)/shard_map/all_gather | solution.py:115
  371.0 768.0 %all-gather.17.cloned.1.call-start = ((), (), s32[]{:S(2)}) async-start(), calls=%async_computation.9 | async-start | bytes 16908288 | tf_op jit(solution)/shard_map/all_gather | solution.py:116
  371.9 1096.8 %all-gather.19.cloned.1.call-start = ((), (), s32[]{:S(2)}) async-start(), calls=%async_computation.10 | async-start | bytes 16908288 | tf_op jit(solution)/shard_map/all_gather | solution.py:117
  372.6 1167.2 %all-gather.21.cloned.1.call-start = ((), (), s32[]{:S(2)}) async-start(), calls=%async_computation.11 | async-start | bytes 2359296 | tf_op jit(solution)/shard_map/all_gather | solution.py:146
  502.7 309.4 %copy-start.32 = (bf16[16,64,128]{2,1,0:T(8,128)(2,1)}, bf16[16,64,128]{2,1,0:T(8,128)(2,1)S(1)}, u32[]{:S(2)}) copy-start(bf16[16,64,128]{2,1,0:T(8,128)(2,1)S(1)} %fusion.75) | copy-start | bytes 786436
  811.1 333.9 %copy-start.88 = (f32[128]{0:T(128)}, f32[128]{0:T(128)S(1)}, u32[]{:S(2)}) copy-start(f32[128]{0:T(128)S(1)} %get-tuple-element.116) | copy-start | bytes 1540
  812.2 332.9 %copy-start.90 = (f32[128]{0:T(128)}, f32[128]{0:T(128)S(1)}, u32[]{:S(2)}) copy-start(f32[128]{0:T(128)S(1)} %get-tuple-element.73) | copy-start | bytes 1540
  812.2 332.8 %copy-start.75 = (f32[128]{0:T(128)}, f32[128]{0:T(128)S(1)}, u32[]{:S(2)}) copy-start(f32[128]{0:T(128)S(1)} %fusion.140) | copy-start | bytes 1540
  1482.8 118.6 %all-gather.25.cloned.1.call-start = ((), (), s32[]{:S(2)}) async-start(), calls=%async_computation.17 | async-start | bytes 2359296 | tf_op jit(solution)/shard_map/all_gather | solution.py:147
  1483.7 274.8 %reduce-scatter.20.cloned.1.call-start = ((), (), s32[]{:S(2)}) async-start(), calls=%async_computation.18 | async-start | bytes 4718592
  1608.3 30.4 copy-start.8
  1608.3 30.4 copy-start.79
  1665.2 233.4 %reduce-scatter.22.cloned.1.call-start = ((), (), s32[]{:S(2)}) async-start(), calls=%async_computation.19 | async-start | bytes 4718592
  1671.3 88.6 %copy-start.25 = (f32[128,1,16,64]{0,3,2,1:T(8,128)S(1)}, f32[128,1,16,64]{0,3,2,1:T(8,128)}, u32[]{:S(2)}) copy-start(f32[128,1,16,64]{0,3,2,1:T(8,128)} %fusion.69) | copy-start | bytes 1572868
  1671.3 88.6 %copy-start.59 = (f32[128,32]{0,1:T(8,128)S(1)}, f32[128,32]{0,1:T(8,128)}, u32[]{:S(2)}) copy-start(f32[128,32]{0,1:T(8,128)} %get-tuple-element.111) | copy-start | bytes 49156
  1807.3 729.9 %reduce-scatter.14.cloned.1.call-start = ((), (), s32[]{:S(2)}) async-start(), calls=%async_computation.13 | async-start | bytes 8454144 | tf_op jit(solution)/shard_map/reduce_scatter | solution.py:278
  1813.7 1408.1 %reduce-scatter.12.cloned.1.call-start = ((), (), s32[]{:S(2)}) async-start(), calls=%async_computation.12 | async-start | bytes 25362432 | tf_op jit(solution)/shard_map/reduce_scatter | solution.py:277
  1823.9 76.1 %copy-start.24 = (f32[128,1,16,64]{0,3,2,1:T(8,128)S(1)}, f32[128,1,16,64]{0,3,2,1:T(8,128)}, u32[]{:S(2)}) copy-start(f32[128,1,16,64]{0,3,2,1:T(8,128)} %fusion.63) | copy-start | bytes 1572868
  1914.4 2042.4 %reduce-scatter.18.cloned.1.call-start = ((), (), s32[]{:S(2)}) async-start(), calls=%async_computation.15 | async-start | bytes 33816576 | tf_op jit(solution)/shard_map/reduce_scatter | solution.py:280
  1942.7 2742.7 %reduce-scatter.16.cloned.1.call-start = ((), (), s32[]{:S(2)}) async-start(), calls=%async_computation.14 | async-start | bytes 33816576 | tf_op jit(solution)/shard_map/reduce_scatter | solution.py:279
  1961.6 72.3 %copy-start.87 = (f32[128]{0:T(128)S(1)}, f32[128]{0:T(128)}, u32[]{:S(2)}) copy-start(f32[128]{0:T(128)} %copy-done.86) | copy-start | bytes 1540
  1961.6 72.3 %copy-start.72 = (f32[2,4,8]{2,1,0:T(4,128)S(1)}, f32[2,4,8]{2,1,0:T(4,128)}, u32[]{:S(2)}) copy-start(f32[2,4,8]{2,1,0:T(4,128)} %param.25) | copy-start | bytes 772
  1961.6 72.3 %copy-start.81 = (f32[2,4,8]{2,1,0:T(4,128)S(1)}, f32[2,4,8]{2,1,0:T(4,128)}, u32[]{:S(2)}) copy-start(f32[2,4,8]{2,1,0:T(4,128)} %param.30) | copy-start | bytes 772
  1961.6 72.3 %copy-start.82 = (f32[2,4,8]{2,1,0:T(4,128)S(1)}, f32[2,4,8]{2,1,0:T(4,128)}, u32[]{:S(2)}) copy-start(f32[2,4,8]{2,1,0:T(4,128)} %param.35) | copy-start | bytes 772
  1961.6 73.0 %copy-start.15 = (f32[128,1,1024]{2,0,1:T(8,128)S(1)}, f32[128,1,1024]{2,0,1:T(8,128)}, u32[]{:S(2)}) copy-start(f32[128,1,1024]{2,0,1:T(8,128)} %copy-done.14) | copy-start | bytes 1572868
  1961.6 575.5 %copy-start.50 = (f32[2,8,1024]{2,1,0:T(8,128)S(1)}, f32[2,8,1024]{2,1,0:T(8,128)}, u32[]{:S(2)}) copy-start(f32[2,8,1024]{2,1,0:T(8,128)} %param.22) | copy-start | bytes 196612
  1961.6 575.5 %copy-start.64 = (f32[2,8,1024]{2,1,0:T(8,128)S(1)}, f32[2,8,1024]{2,1,0:T(8,128)}, u32[]{:S(2)}) copy-start(f32[2,8,1024]{2,1,0:T(8,128)} %param.27) | copy-start | bytes 196612
  1961.6 575.5 %copy-start.65 = (f32[2,8,1024]{2,1,0:T(8,128)S(1)}, f32[2,8,1024]{2,1,0:T(8,128)}, u32[]{:S(2)}) copy-start(f32[2,8,1024]{2,1,0:T(8,128)} %param.32) | copy-start | bytes 196612
  1966.8 1255.0 %copy-start.44 = (f32[2,8,3072]{2,1,0:T(8,128)S(1)}, f32[2,8,3072]{2,1,0:T(8,128)}, u32[]{:S(2)}) copy-start(f32[2,8,3072]{2,1,0:T(8,128)} %param.21) | copy-start | bytes 589828
  1966.8 1255.0 %copy-start.57 = (f32[2,8,3072]{2,1,0:T(8,128)S(1)}, f32[2,8,3072]{2,1,0:T(8,128)}, u32[]{:S(2)}) copy-start(f32[2,8,3072]{2,1,0:T(8,128)} %param.26) | copy-start | bytes 589828
  1966.8 1255.0 %copy-start.58 = (f32[2,8,3072]{2,1,0:T(8,128)S(1)}, f32[2,8,3072]{2,1,0:T(8,128)}, u32[]{:S(2)}) copy-start(f32[2,8,3072]{2,1,0:T(8,128)} %param.31) | copy-start | bytes 589828
  1966.9 1989.9 %copy-start.35 = (f32[2,32,1024]{2,1,0:T(8,128)S(1)}, f32[2,32,1024]{2,1,0:T(8,128)}, u32[]{:S(2)}) copy-start(f32[2,32,1024]{2,1,0:T(8,128)} %param.24) | copy-start | bytes 786436
  1966.9 1989.9 %copy-start.45 = (f32[2,32,1024]{2,1,0:T(8,128)S(1)}, f32[2,32,1024]{2,1,0:T(8,128)}, u32[]{:S(2)}) copy-start(f32[2,32,1024]{2,1,0:T(8,128)} %param.29) | copy-start | bytes 786436
  1966.9 1989.9 %copy-start.46 = (f32[2,32,1024]{2,1,0:T(8,128)S(1)}, f32[2,32,1024]{2,1,0:T(8,128)}, u32[]{:S(2)}) copy-start(f32[2,32,1024]{2,1,0:T(8,128)} %param.34) | copy-start | bytes 786436
  2035.5 2649.8 %copy-start.37 = (f32[2,8,4096]{2,1,0:T(8,128)S(1)}, f32[2,8,4096]{2,1,0:T(8,128)}, u32[]{:S(2)}) copy-start(f32[2,8,4096]{2,1,0:T(8,128)} %param.23) | copy-start | bytes 786436
  2035.5 2649.8 %copy-start.47 = (f32[2,8,4096]{2,1,0:T(8,128)S(1)}, f32[2,8,4096]{2,1,0:T(8,128)}, u32[]{:S(2)}) copy-start(f32[2,8,4096]{2,1,0:T(8,128)} %param.28) | copy-start | bytes 786436
  2035.5 2649.8 %copy-start.48 = (f32[2,8,4096]{2,1,0:T(8,128)S(1)}, f32[2,8,4096]{2,1,0:T(8,128)}, u32[]{:S(2)}) copy-start(f32[2,8,4096]{2,1,0:T(8,128)} %param.33) | copy-start | bytes 786436
  (73 other events, 400.6 us)
Sparse Core Ops, SparseCore 0:
  10.3 325.7 all-gather.10
  369.5 65.7 all-gather.12
  437.5 59.3 all-gather.22
  499.1 309.8 all-gather.14
  811.1 327.8 all-gather.16
  1141.1 327.5 all-gather.18
  1483.0 56.8 all-gather.20
  1542.0 59.3 all-gather.24
  1665.3 93.0 reduce-scatter.19
  1807.4 91.2 reduce-scatter.21
  1901.0 636.1 reduce-scatter.13
  2539.6 682.2 reduce-scatter.11
  3224.4 732.3 reduce-scatter.17
  3959.2 726.1 reduce-scatter.15
where the time goes:
time: 4700 us; the launch traced here: 4690 us
  waiting for transfers between devices  3980 us (85%)
  blocking collectives  373 us (8%)
  matrix products  159 us (3%)
  local copies, waits for them, and re-layouts  92.8 us (2%)
  other arithmetic  71.6 us (2%)
    reduce_scatter x1, waiting for transfers between devices, body(): lax.psum_scatter(summed[3], ('dp', 'seq'), scatter_dimension=1, tiled=True)  733 us
    reduce_scatter x1, waiting for transfers between devices, body(): lax.psum_scatter(summed[2], ('dp', 'seq'), scatter_dimension=1, tiled=True)  727 us
    reduce_scatter x1, waiting for transfers between devices, body(): lax.psum_scatter(summed[0], ('dp', 'seq'), scatter_dimension=1, tiled=True)  683 us
    reduce_scatter x1, waiting for transfers between devices, body(): lax.psum_scatter(summed[1], ('dp', 'seq'), scatter_dimension=1, tiled=True)  502 us
    all_gather x1, waiting for transfers between devices, body(): lax.all_gather(w_up.astype(jnp.bfloat16), ('dp', 'seq'), axis=1, tiled=True)  327 us
    all_gather x1, waiting for transfers between devices, body(): lax.all_gather(w_down.astype(jnp.bfloat16), ('dp', 'seq'), axis=1, tiled=...  324 us
    all_gather x1, waiting for transfers between devices, body(): lax.all_gather(w_out.astype(jnp.bfloat16), ('dp', 'seq'), axis=1, tiled=T...  306 us
    all_gather x1, blocking collectives, body(): lax.all_gather(gains.astype(jnp.bfloat16), ('dp', 'seq'), axis=2, tiled=T...  306 us
  transfers between devices with their start and end apart: 14, of which 13 were waited for; matrix products, arithmetic and copies ran while one was open for 3% of the time, Pallas kernels for 0%

commit v1 on v0

v1 whole, which is shorter than its diff:
```python
import jax
import jax.numpy as jnp
from jax import lax
from jax.experimental import pallas as pl
from jax.experimental.pallas import tpu as pltpu
from jax.sharding import Mesh
from jax.sharding import PartitionSpec as P

D = 1024
HEADS = 16
HEAD_DIM = 64
FF = 4096
LAYERS = 2
STEP = 5
LENGTH = 1024
BLOCK = 128
QB = 256

norm_eps = 1e-05
beta_first = 0.9
beta_second = 0.95
adam_eps = 1e-08
weight_decay = 0.1
rate_matrix = 0.04
rate_gain = 0.4
masked_score = -1e30
score_scale = HEAD_DIM ** (-0.5)

bf16 = jnp.bfloat16
f32 = jnp.float32
SEQ = ("y", "zl")
DP = ("zh", "x", "c")
ZAX = ("zh", "zl")
XY = ("x", "y")
ALL = ("zh", "x", "c", "y", "zl")


def dot(a, b, dims):
    return lax.dot_general(a, b, (dims, ((), ())), preferred_element_type=f32)


def mm(a, b):
    return dot(a, b, ((1,), (0,)))


def mm_nt(a, b):
    return dot(a, b, ((1,), (1,)))


def mm_tn(a, b):
    return dot(a, b, ((0,), (0,)))


def swap_halves(x):
    lane = lax.broadcasted_iota(jnp.int32, x.shape, 1)
    return jnp.where((lane % 64) < 32, pltpu.roll(x, 96, 1), pltpu.roll(x, 32, 1))


def lane_mask(x, row):
    lane = lax.broadcasted_iota(jnp.int32, x.shape, 1)
    return jnp.where((lane // 64) == row, x, jnp.zeros_like(x))


def allowed_mask(start_row, keys, first_query):
    key = lax.broadcasted_iota(jnp.int32, (keys, QB), 0)
    query = lax.broadcasted_iota(jnp.int32, (keys, QB), 1) + first_query
    return (key >= start_row) & (key <= query)


def att_fwd_kernel(qkv_ref, cos_ref, sin_ref, start_ref, att_ref, lse_ref, rot_ref, att_t):
    cosine = cos_ref[...]
    sine = sin_ref[...]
    q = qkv_ref[:, 0:128].astype(f32)
    k = qkv_ref[:, 128:256].astype(f32)
    v = qkv_ref[:, 256:384]
    q = q * cosine + swap_halves(q) * sine
    k = k * cosine + swap_halves(k) * sine
    rot_ref[:, 0:128] = q.astype(bf16)
    rot_ref[:, 128:256] = k.astype(bf16)
    rot_ref[:, 256:384] = v
    v_t = jnp.transpose(v.astype(f32)).astype(bf16)
    for row in range(2):
        k_row = lane_mask(k, row).astype(bf16)
        for step in range(LENGTH // QB):
            first = step * QB
            keys = first + QB
            q_blk = rot_ref[first : first + QB, 0:128]
            s = mm_nt(k_row[:keys], q_blk) * score_scale
            ok = allowed_mask(start_ref[row : row + 1, first : first + QB], keys, first)
            s = jnp.where(ok, s, masked_score)
            top = jnp.max(s, axis=0, keepdims=True)
            e = jnp.exp(s - top)
            total = jnp.sum(e, axis=0, keepdims=True)
            lse_ref[row : row + 1, first : first + QB] = top + jnp.log(total)
            p = (e * (1.0 / total)).astype(bf16)
            att_t[row * 64 : row * 64 + 64, first : first + QB] = mm(
                v_t[row * 64 : row * 64 + 64, :keys], p
            )
    att_ref[...] = jnp.transpose(att_t[...]).astype(bf16)


def att_bwd_kernel(rot_ref, datt_ref, lse_ref, cos_ref, sin_ref, start_ref, out_ref, dk_acc, dv_acc, dq_t):
    cosine = cos_ref[...]
    sine = sin_ref[...]
    q = rot_ref[:, 0:128]
    k = rot_ref[:, 128:256]
    v = rot_ref[:, 256:384]
    datt = datt_ref[...]
    k_t = jnp.transpose(k.astype(f32)).astype(bf16)
    dk_acc[...] = jnp.zeros_like(dk_acc)
    dv_acc[...] = jnp.zeros_like(dv_acc)
    for row in range(2):
        q_row = lane_mask(q, row)
        datt_row = lane_mask(datt, row)
        for step in range(LENGTH // QB):
            first = step * QB
            keys = first + QB
            q_blk = q_row[first : first + QB]
            datt_blk = datt_row[first : first + QB]
            s = mm_nt(k[:keys], q_blk) * score_scale
            ok = allowed_mask(start_ref[row : row + 1, first : first + QB], keys, first)
            p = jnp.where(ok, jnp.exp(s - lse_ref[row : row + 1, first : first + QB]), 0.0)
            dp = mm_nt(v[:keys], datt_blk)
            delta = jnp.sum(p * dp, axis=0, keepdims=True)
            ds = (p * (dp - delta)).astype(bf16)
            dq_t[row * 64 : row * 64 + 64, first : first + QB] = mm(
                k_t[row * 64 : row * 64 + 64, :keys], ds
            )
            dk_acc[0:keys, :] += mm(ds, q_blk)
            dv_acc[0:keys, :] += mm(p.astype(bf16), datt_blk)
    dq = jnp.transpose(dq_t[...]) * score_scale
    dk = dk_acc[...] * score_scale
    out_ref[:, 0:128] = (dq * cosine - swap_halves(dq) * sine).astype(bf16)
    out_ref[:, 128:256] = (dk * cosine - swap_halves(dk) * sine).astype(bf16)
    out_ref[:, 256:384] = dv_acc[...].astype(bf16)


def whole(count):
    return [pl.BlockSpec(memory_space=pltpu.VMEM)] * count


def att_forward(qkv, cosine, sine, starts):
    return pl.pallas_call(
        att_fwd_kernel,
        out_shape=(
            jax.ShapeDtypeStruct((LENGTH, 128), bf16),
            jax.ShapeDtypeStruct((8, LENGTH), f32),
            jax.ShapeDtypeStruct((LENGTH, 384), bf16),
        ),
        in_specs=whole(4),
        out_specs=tuple(whole(3)),
        scratch_shapes=[pltpu.VMEM((128, LENGTH), f32)],
        compiler_params=pltpu.CompilerParams(vmem_limit_bytes=16 * 1024 * 1024),
        name="att_forward",
    )(qkv, cosine, sine, starts)


def att_backward(rot, datt, lse, cosine, sine, starts):
    return pl.pallas_call(
        att_bwd_kernel,
        out_shape=jax.ShapeDtypeStruct((LENGTH, 384), bf16),
        in_specs=whole(6),
        out_specs=whole(1)[0],
        scratch_shapes=[
            pltpu.VMEM((LENGTH, 128), f32),
            pltpu.VMEM((LENGTH, 128), f32),
            pltpu.VMEM((128, LENGTH), f32),
        ],
        compiler_params=pltpu.CompilerParams(vmem_limit_bytes=16 * 1024 * 1024),
        name="att_backward",
    )(rot, datt, lse, cosine, sine, starts)


def rms_scale(values):
    return lax.rsqrt(jnp.mean(values * values, axis=-1, keepdims=True) + norm_eps)


def rms_norm(values, gain_row):
    return values * rms_scale(values) * gain_row


def rms_back(values, gain_row, grad):
    scale = rms_scale(values)
    unit = values * scale
    scaled = grad * gain_row
    inner = jnp.mean(scaled * unit, axis=-1, keepdims=True)
    return scale * (scaled - unit * inner), jnp.sum(grad * unit, axis=0)


def adam_update(master, moment_one, moment_two, gradient, rate, decay):
    moment_new = beta_first * moment_one + (1.0 - beta_first) * gradient
    square_new = beta_second * moment_two + (1.0 - beta_second) * gradient * gradient
    moment_hat = moment_new / (1.0 - beta_first**STEP)
    square_hat = square_new / (1.0 - beta_second**STEP)
    updated = master - rate * (moment_hat / (jnp.sqrt(square_hat) + adam_eps) + decay * master)
    return (updated, moment_new, square_new)


def other_core(x):
    return lax.ppermute(x, "c", [(0, 1), (1, 0)])


def both_rows(x):
    return jnp.concatenate([x, other_core(x)], axis=0)


def own_sum(part):
    sent = other_core(part[BLOCK:].astype(bf16))
    return part[:BLOCK] + sent.astype(f32)


def seq_swap(x):
    return lax.all_to_all(x, SEQ, 0, 0, tiled=True)


CUBE, PLANE, LINE = 0, 3, 4
QKV, OUT, UP, DOWN, GAIN = "qkv", "out", "up", "down", "gain"
WIDTH = {QKV: 1536, OUT: 512, UP: 2048, DOWN: 2048, GAIN: 128}
SHAPE = {QKV: (1024, 1536), OUT: (512, 1024), UP: (1024, 2048), DOWN: (2048, 1024), GAIN: (1024, 128)}


def place(i):
    return (i // 64) * 2 + i % 2, (i // 16) % 4, (i // 8) % 2, (i // 2) % 4


def device_at(z, x, c, y):
    return (((z // 2) * 4 + x) * 2 + c) * 8 + y * 2 + z % 2


def pairs(axis, phase):
    found = []
    for i in range(128):
        z, x, c, y = place(i)
        mask = 3 if (c if phase else 1 - c) else 1
        x, y, z = (x ^ mask, y, z) if axis == 0 else (x, y ^ mask, z) if axis == 1 else (x, y, z ^ mask)
        found.append((i, device_at(z, x, c, y)))
    return found


PAIRS = {(axis, phase): pairs(axis, phase) for axis in range(3) for phase in range(2)}


def pair_swap(x, axis, phase):
    return lax.ppermute(x, ALL, PAIRS[axis, phase])


def add_low(a, b):
    return (a.astype(f32) + b.astype(f32)).astype(bf16)


def cube_groups():
    found = {}
    for i in range(128):
        z, x, c, y = place(i)
        shift, mask = (0, 1) if c else (1, 3)
        rank = ((x >> shift) & 1) * 4 + ((y >> shift) & 1) * 2 + ((z >> shift) & 1)
        key = (c,) + tuple(min(v, v ^ mask) for v in (x, y, z))
        found.setdefault(key, [0] * 8)[rank] = i
    return list(found.values())


CUBES = cube_groups()


def cube_all_to_all(x):
    return lax.all_to_all(x, ALL, 0, 0, axis_index_groups=CUBES, tiled=True)


def cube_round(cur, k):
    return [pair_swap(cur[g], (g + k) % 3, 1) for g in range(3)]


def join(cur, got):
    return [jnp.concatenate([x, y], axis=0) for x, y in zip(cur, got)]


def scatter_round(keep, send, k):
    cur = [add_low(x, y) for x, y in zip(keep, cube_round(send, k))]
    half = cur[0].shape[0] // 2
    return [x[:half] for x in cur], [x[half:] for x in cur]


def together(*values):
    return lax.optimization_barrier(values)


def unit_tables(mine):
    my_z, my_x, core, my_y = mine
    first = jnp.where(core == 0, 3, 1)
    last = jnp.where(core == 0, 1, 3)
    shift = jnp.where(core == 0, 1, 0)
    p = jnp.arange(64, dtype=jnp.int32)
    rows = []
    for g in range(5):
        if g < 3:
            at = [my_x, my_y, my_z]
            for k in range(3):
                at[(g + k) % 3] = at[(g + k) % 3] ^ (((p >> (3 + k)) & 1) * last)
            for axis in range(3):
                differs = ((at[axis] >> shift) & 1) ^ ((p >> (2 - axis)) & 1)
                at[axis] = at[axis] ^ (differs * first)
            x, y, z = at
        else:
            plane, line = (p >> 2, p & 3) if g == 3 else (p & 15, p >> 4)
            x, y = plane >> 2, plane & 3
            z = my_z ^ ((line & 1) * last) ^ ((line >> 1) * first)
        zh, zl = z >> 1, z & 1
        rows += [
            (((zh * 4 + x) * 2 + zl) * 4 + y) * 16,
            ((zh * 4 + x) * 4 + y) * 16,
            zl * 512,
            (((zh * 4 + x) * 4 + y) * 2 + zl) * 32,
        ]
    return jnp.stack(rows).astype(jnp.int32)


def segments(names, bounds):
    pieces = []
    start = 0
    for name in names:
        for part in range(2 if name == DOWN else 1):
            width = 1024 if name == DOWN else WIDTH[name]
            pieces.append((name, start, width, 16 * part))
            start += width
    found = []
    for a, b in bounds:
        group = []
        for name, first, width, extra in pieces:
            lo, hi = max(a, first), min(b, first + width)
            if lo < hi:
                group.append((name, lo - a, lo - first, hi - lo, extra))
        found.append(group)
    return found


def whole_slice(tab, ref, name, group, p, column, count, extra):
    if name == OUT:
        row = pl.multiple_of(tab[4 * group + 1, p], 16)
        col = pl.multiple_of(tab[4 * group + 2, p] + column, 128)
        return ref.at[pl.ds(row, 16), pl.ds(col, count)]
    if name == DOWN:
        row = pl.multiple_of(tab[4 * group + 3, p] + extra, 16)
    else:
        row = pl.multiple_of(tab[4 * group, p], 16)
    return ref.at[pl.ds(row, 16), pl.ds(column, count)]


def unpack(names, bounds, groups, tables, order):
    plan = segments(names, bounds)
    per = len(groups[0])
    flat = [buffer for group in groups for buffer in group]

    def kernel(tab, *refs):
        sources = refs[: len(flat)]
        targets = dict(zip(names, refs[len(flat) : len(flat) + len(names)]))
        sems = refs[-1]

        def step(i, carry):
            for g, group in enumerate(plan):
                for part in range(per):
                    for name, at, column, count, extra in group:
                        pltpu.make_async_copy(
                            sources[g * per + part].at[i, :, pl.ds(at, count)],
                            whole_slice(tab, targets[name], name, order + g, i + part * (64 // per), column, count, extra),
                            sems.at[names.index(name)],
                        ).start()
            return carry

        lax.fori_loop(0, 64 // per, step, 0)
        for n, name in enumerate(names):
            pltpu.make_async_copy(targets[name], targets[name], sems.at[n]).wait()

    return pl.pallas_call(
        kernel,
        out_shape=tuple(jax.ShapeDtypeStruct(SHAPE[name], bf16) for name in names),
        in_specs=[pl.BlockSpec(memory_space=pltpu.SMEM)] + [pl.BlockSpec(memory_space=pl.ANY)] * len(flat),
        out_specs=tuple(whole(len(names))),
        scratch_shapes=[pltpu.SemaphoreType.DMA((len(names),))],
        compiler_params=pltpu.CompilerParams(vmem_limit_bytes=20 * 1024 * 1024),
        name="unpack",
    )(tables, *flat)


def pack(names, bounds, weights, tables, order):
    plan = segments(names, bounds)
    per = 2 if order == CUBE else 1
    shapes = [(64 // per, 16, b - a) for a, b in bounds for _ in range(per)]

    def kernel(tab, *refs):
        sources = dict(zip(names, refs[: len(names)]))
        targets = refs[len(names) : len(names) + len(shapes)]
        sems = refs[-1]

        def step(i, carry):
            for g, group in enumerate(plan):
                for part in range(per):
                    for name, at, column, count, extra in group:
                        pltpu.make_async_copy(
                            whole_slice(tab, sources[name], name, order + g, i + part * (64 // per), column, count, extra),
                            targets[g * per + part].at[i, :, pl.ds(at, count)],
                            sems.at[g * per + part],
                        ).start()
            return carry

        lax.fori_loop(0, 64 // per, step, 0)
        for n in range(len(shapes)):
            pltpu.make_async_copy(targets[n], targets[n], sems.at[n]).wait()

    out = pl.pallas_call(
        kernel,
        out_shape=tuple(jax.ShapeDtypeStruct(shape, bf16) for shape in shapes),
        in_specs=[pl.BlockSpec(memory_space=pltpu.SMEM)] + whole(len(names)),
        out_specs=tuple([pl.BlockSpec(memory_space=pl.ANY)] * len(shapes)),
        scratch_shapes=[pltpu.SemaphoreType.DMA((len(shapes),))],
        compiler_params=pltpu.CompilerParams(vmem_limit_bytes=20 * 1024 * 1024),
        name="pack",
    )(tables, *weights)
    return [out[g * per : (g + 1) * per] for g in range(len(bounds))]


def plane_gather(space):
    cur = space[None]
    for phase in (1, 0):
        cur = jnp.concatenate([cur, pair_swap(cur, 2, phase)], axis=0)
    return lax.all_gather(cur, XY, axis=0, tiled=True)


def plane_scatter(buffer):
    cur = lax.psum_scatter(buffer.reshape(1024, -1), XY, scatter_dimension=0, tiled=True).reshape(4, 16, -1)
    for phase in (0, 1):
        half = cur.shape[0] // 2
        cur = add_low(cur[:half], pair_swap(cur[half:], 2, phase))
    return cur[0]


CROSS = {
    flip: [
        (device_at(z, x, c, y), device_at((z // 2) * 2 + c, x, (z % 2) ^ flip, y))
        for z in range(4)
        for x in range(4)
        for c in range(2)
        for y in range(4)
    ]
    for flip in range(2)
}
CROSS_BACK = {flip: [(b, a) for a, b in CROSS[flip]] for flip in range(2)}


def rows_to_units(halves, zl, core):
    near = lax.ppermute(jnp.where(zl == 0, halves[0], halves[1]), ALL, CROSS[0])
    far = lax.ppermute(jnp.where(zl == 0, halves[1], halves[0]), ALL, CROSS[1])
    return jnp.where(core == 0, jnp.concatenate([near, far], axis=0), jnp.concatenate([far, near], axis=0))


def units_to_rows(units, zl, core):
    near = lax.ppermute(jnp.where(core == 0, units[:8], units[8:]), ALL, CROSS_BACK[0])
    far = lax.ppermute(jnp.where(core == 0, units[8:], units[:8]), ALL, CROSS_BACK[1])
    return jnp.where(zl == 0, jnp.stack([near, far]), jnp.stack([far, near]))


def zl_swap(x):
    return lax.ppermute(x, "zl", [(0, 1), (1, 0)])


def out_to_unit(out, zl):
    low, high = out[..., :512], out[..., 512:]
    kept = jnp.where(zl == 0, low, high)
    got = zl_swap(jnp.where(zl == 0, high, low))
    return jnp.where(zl == 0, jnp.concatenate([kept, got], axis=1), jnp.concatenate([got, kept], axis=1))


def out_to_rows(units, zl):
    top, bottom = units[:, :8], units[:, 8:]
    kept = jnp.where(zl == 0, top, bottom)
    got = zl_swap(jnp.where(zl == 0, bottom, top))
    return jnp.where(zl == 0, jnp.concatenate([kept, got], axis=-1), jnp.concatenate([got, kept], axis=-1))


ATTN_NAMES = (QKV, OUT, GAIN)
ATTN_CUTS = ((0, 768), (768, 1536), (1536, 2176))
ZERO_NAMES = (QKV, OUT, GAIN, UP, DOWN)
ZERO_CUTS = ((0, 2176), (2176, 4224), (4224, 6272))
MLP_NAMES = (UP, DOWN)
LAYER_NAMES = (QKV, OUT, UP, DOWN)
LAYER_CUTS = ((0, 6144),)


def body(
    tokens,
    cotangent,
    lengths,
    w_qkv,
    w_out,
    w_up,
    w_down,
    gains,
    moment_qkv,
    moment_out,
    moment_up,
    moment_down,
    moment_gains,
    square_qkv,
    square_out,
    square_up,
    square_down,
    square_gains,
):
    core = lax.axis_index("c")
    zl = lax.axis_index("zl")
    my_z = lax.axis_index("zh") * 2 + zl
    tables = unit_tables((my_z, lax.axis_index("x"), core, lax.axis_index("y")))

    both = jnp.concatenate([lengths, other_core(lengths)], axis=0)
    ends = jnp.cumsum(both, axis=-1)
    starts = ends - both
    places = jnp.arange(LENGTH, dtype=jnp.int32)
    doc_ids = jnp.sum((places[None, :, None] >= ends[:, None, :]).astype(jnp.int32), axis=-1)
    picked = doc_ids[:, :, None] == jnp.arange(4, dtype=jnp.int32)[None, None, :]
    first_place = jnp.sum(jnp.where(picked, starts[:, None, :], 0), axis=-1)
    positions = (places[None, :] - first_place).astype(f32)
    inverse = 10000.0 ** (-jnp.arange(32, dtype=f32) / 32)
    angle = positions[:, :, None] * inverse
    cos_half = jnp.cos(angle)
    sin_half = jnp.sin(angle)
    cosine = jnp.concatenate([cos_half[0], cos_half[0], cos_half[1], cos_half[1]], axis=-1)
    sine = jnp.concatenate([-sin_half[0], sin_half[0], -sin_half[1], sin_half[1]], axis=-1)
    start_rows = jnp.concatenate([first_place, jnp.zeros((6, LENGTH), jnp.int32)], axis=0)

    qkv_halves = w_qkv.astype(bf16).reshape(LAYERS, 8, 3, 8, 2, 64).transpose(4, 1, 0, 3, 2, 5).reshape(2, 8, LAYERS * 1536)
    up_halves = w_up.astype(bf16).reshape(LAYERS, 8, 8, 2, 256).transpose(3, 1, 0, 2, 4).reshape(2, 8, LAYERS * 2048)
    gain_rows = gains.astype(bf16).reshape(8, 8).T
    gain_rows = jnp.broadcast_to(jnp.pad(gain_rows, ((0, 0), (0, 120)))[None], (2, 8, 128))
    units = rows_to_units(jnp.concatenate([qkv_halves, up_halves, gain_rows], axis=-1), zl, core)
    qkv_units, up_units, gain_units = units[:, :3072], units[:, 3072:7168], units[:, 7168:]
    out_units = out_to_unit(w_out.astype(bf16), zl)
    down_units = w_down.astype(bf16).reshape(LAYERS, 2, 16, 1024).transpose(0, 2, 1, 3).reshape(LAYERS, 16, 2048)
    attn_space = jnp.concatenate([qkv_units[:, :1536], out_units[0], gain_units], axis=-1)
    mlp_space = jnp.concatenate([up_units[:, :2048], down_units[0]], axis=-1)
    layer_space = jnp.concatenate([qkv_units[:, 1536:], out_units[1], up_units[:, 2048:], down_units[1]], axis=-1)
    zero_space = jnp.concatenate([attn_space, mlp_space], axis=-1)
    zero_space, cosine, sine, start_rows = together(zero_space, cosine, sine, start_rows)
    line = layer_space[None]
    line_got = pair_swap(line, 2, 1)
    eight = cube_all_to_all(jnp.broadcast_to(zero_space[None], (8,) + zero_space.shape))
    line, line_got, eight = together(line, line_got, eight)
    line = jnp.concatenate([line, line_got], axis=0)
    cur = [eight[..., a:b] for a, b in ZERO_CUTS]
    line, line_got, got = together(line, pair_swap(line, 2, 0), cube_round(cur, 0))
    line = jnp.concatenate([line, line_got], axis=0)
    cur = join(cur, got)
    cur = join(cur, cube_round(cur, 1))
    got = cube_round(cur, 2)
    line, got = together(line, got)
    layer_buffer = lax.all_gather(line, XY, axis=0, tiled=True)
    zero_groups = list(zip(cur, got))
    qkv_zero, out_zero, gain_whole, up_zero, down_zero = unpack(ZERO_NAMES, ZERO_CUTS, zero_groups, tables, CUBE)
    gain_all = gain_whole[:, :8].astype(f32).T.reshape(LAYERS, 4, D)

    hidden = tokens.reshape(BLOCK, D).astype(f32)
    kept = []
    for l in range(LAYERS):
        gain = gain_all[l]
        if l == 0:
            weight_qkv, weight_out, weight_up, weight_down = qkv_zero, out_zero, up_zero, down_zero
        else:
            weight_qkv, weight_out, weight_up, weight_down = unpack(
                LAYER_NAMES, LAYER_CUTS, [(layer_buffer,)], tables, PLANE
            )
        layer_input = hidden
        normed = both_rows(rms_norm(hidden, gain[0]).astype(bf16))
        mixed = mm(normed, weight_qkv).astype(bf16)
        mixed = mixed.reshape(2, BLOCK, 8, 3, 64).transpose(2, 1, 3, 0, 4).reshape(8, BLOCK, 384)
        mixed = seq_swap(mixed).reshape(LENGTH, 384)
        att_mine, lse, rot = att_forward(mixed, cosine, sine, start_rows)
        att = seq_swap(att_mine.reshape(8, BLOCK, 128))
        att = att.reshape(8, BLOCK, 2, 64).transpose(2, 1, 0, 3).reshape(2 * BLOCK, 512)
        branch = own_sum(mm(att, weight_out))
        middle = hidden + rms_norm(branch, gain[1])
        normed_mlp = both_rows(rms_norm(middle, gain[2]).astype(bf16))
        upward = mm(normed_mlp, weight_up)
        active = jax.nn.gelu(upward, approximate=False).astype(bf16)
        downward = own_sum(mm(active, weight_down))
        hidden = middle + rms_norm(downward, gain[3])
        kept.append(
            (
                layer_input,
                normed,
                rot,
                lse,
                att,
                branch,
                middle,
                normed_mlp,
                upward,
                active,
                downward,
                weight_qkv,
                weight_out,
                weight_up,
                weight_down,
            )
        )
    output = hidden.astype(bf16)

    grad_hidden = cotangent.reshape(BLOCK, D).astype(f32)
    gain_grads = [None] * LAYERS
    for l in reversed(range(LAYERS)):
        (
            layer_input,
            normed,
            rot,
            lse,
            att,
            branch,
            middle,
            normed_mlp,
            upward,
            active,
            downward,
            weight_qkv,
            weight_out,
            weight_up,
            weight_down,
        ) = kept[l]
        gain = gain_all[l]
        d_down, grad_three = rms_back(downward, gain[3], grad_hidden)
        d_down = both_rows(d_down.astype(bf16))
        d_active = mm_nt(d_down, weight_down)
        _, gelu_back = jax.vjp(lambda u: jax.nn.gelu(u, approximate=False), upward)
        d_up = gelu_back(d_active)[0].astype(bf16)
        d_normed = own_sum(mm_nt(d_up, weight_up))
        grad_wdown = mm_tn(active, d_down).astype(bf16)
        grad_wup = mm_tn(normed_mlp, d_up).astype(bf16)
        if l == 1:
            mlp_pack = pack(MLP_NAMES, ((0, 4096),), (grad_wup, grad_wdown), tables, PLANE)[0][0]
            mlp_pack, d_normed = together(mlp_pack, d_normed)
            mlp_own = plane_scatter(mlp_pack)
        else:
            mid_pack = pack(LAYER_NAMES, LAYER_CUTS, held + (grad_wup, grad_wdown), tables, PLANE)[0][0]
            mid_pack, d_normed = together(mid_pack, d_normed)
            mid_own = plane_scatter(mid_pack)
        d_middle, grad_two = rms_back(middle, gain[2], d_normed)
        d_middle = d_middle + grad_hidden
        d_branch, grad_one = rms_back(branch, gain[1], d_middle)
        d_branch = both_rows(d_branch.astype(bf16))
        d_att = mm_nt(d_branch, weight_out).astype(bf16)
        d_att = d_att.reshape(2, BLOCK, 8, 64).transpose(2, 1, 0, 3).reshape(8, BLOCK, 128)
        d_att = seq_swap(d_att).reshape(LENGTH, 128)
        grad_wout = mm_tn(att, d_branch).astype(bf16)
        d_mixed = att_backward(rot, d_att, lse, cosine, sine, start_rows)
        d_mixed = seq_swap(d_mixed.reshape(8, BLOCK, 384))
        d_mixed = d_mixed.reshape(8, BLOCK, 3, 2, 64).transpose(3, 1, 0, 2, 4).reshape(2 * BLOCK, 1536)
        grad_wqkv = mm_tn(normed, d_mixed).astype(bf16)
        held = (grad_wqkv, grad_wout)
        d_normed = own_sum(mm_nt(d_mixed, weight_qkv))
        d_input, grad_zero = rms_back(layer_input, gain[0], d_normed)
        grad_hidden = d_input + d_middle
        gain_grads[l] = jnp.stack([grad_zero, grad_one, grad_two, grad_three])
    input_grad = grad_hidden.astype(bf16)

    gain_sum = jnp.pad(jnp.stack(gain_grads).reshape(8, D).T.astype(bf16), ((0, 0), (0, 120)))
    tail_pack = pack(ATTN_NAMES, ATTN_CUTS, (grad_wqkv, grad_wout, gain_sum), tables, CUBE)
    tail = [x[0] for x in tail_pack], [x[1] for x in tail_pack]
    for k in (2, 1, 0):
        tail = scatter_round(*tail, k)
    tail_own = jnp.concatenate([jnp.concatenate(x, axis=-1) for x in tail], axis=0)
    tail_own = jnp.sum(cube_all_to_all(tail_own).astype(f32), axis=0).astype(bf16)

    g_out_units = jnp.stack([tail_own[:, 1536:2048], mid_own[:, 1536:2048]])
    g_down = jnp.stack([mid_own[:, 4096:], mlp_own[:, 2048:]])
    g_down = g_down.reshape(LAYERS, 16, 2, 1024).transpose(0, 2, 1, 3).reshape(LAYERS, 32, 1024).astype(f32)
    both = jnp.concatenate(
        [tail_own[:, :1536], mid_own[:, :1536], mid_own[:, 2048:4096], mlp_own[:, :2048], tail_own[:, 2048:]], axis=-1
    )
    both, g_out_units = together(both, g_out_units)
    g_out = out_to_rows(g_out_units, zl).astype(f32)
    both = units_to_rows(both, zl, core).astype(f32)
    g_qkv = both[..., :3072].reshape(2, 8, LAYERS, 8, 3, 64).transpose(2, 1, 4, 3, 0, 5).reshape(LAYERS, 8, 3 * D)
    g_up = both[..., 3072:7168].reshape(2, 8, LAYERS, 8, 256).transpose(2, 1, 3, 0, 4).reshape(LAYERS, 8, FF)
    g_gain = jnp.sum(both[:, :, 7168:7176], axis=0).T.reshape(LAYERS, 4, 8)

    upd_qkv = adam_update(w_qkv, moment_qkv, square_qkv, g_qkv, rate_matrix, weight_decay)
    upd_out = adam_update(w_out, moment_out, square_out, g_out, rate_matrix, weight_decay)
    upd_up = adam_update(w_up, moment_up, square_up, g_up, rate_matrix, weight_decay)
    upd_down = adam_update(w_down, moment_down, square_down, g_down, rate_matrix, weight_decay)
    upd_gains = adam_update(gains, moment_gains, square_gains, g_gain, rate_gain, 0.0)
    updates = (upd_qkv, upd_out, upd_up, upd_down, upd_gains)
    return (
        output.reshape(BLOCK, 1, D),
        input_grad.reshape(BLOCK, 1, D),
        *(u[0] for u in updates),
        *(u[1] for u in updates),
        *(u[2] for u in updates),
        *(u[0].astype(bf16) for u in updates),
    )


def solution(mesh):
    fine = Mesh(mesh.devices.reshape(2, 4, 2, 4, 2), ("zh", "x", "c", "y", "zl"))
    tokens_spec = P(SEQ, DP, None)
    rows_spec = P(None, DP + SEQ, None)
    gains_spec = P(None, None, DP + SEQ)
    masters = (rows_spec,) * 4 + (gains_spec,)
    return jax.shard_map(
        body,
        mesh=fine,
        in_specs=(tokens_spec, tokens_spec, P(DP, None)) + masters * 3,
        out_specs=(tokens_spec, tokens_spec) + masters * 4,
        check_vma=False,
    )
```

time: 4700 us -> 574 us (0.12)
  waiting for transfers between devices: 3980 us -> 163 us
  blocking collectives: 373 us -> 98.7 us
  matrix products: 159 us -> 40.4 us
  starting transfers between devices: 1.43 us -> 87.9 us
  Pallas kernels: 0 us -> 60.3 us
    reduce_scatter x4 -> x2, waiting for transfers between devices: 2640 us -> 0.02 us  [plane_scatter(): lax.psum_scatter(buffer.reshape(1024, -1), XY, scatter_dimension=0, tiled...]
    all_gather x8 -> x1, waiting for transfers between devices: 1170 us -> 27.1 us  [body(): layer_buffer = lax.all_gather(line, XY, axis=0, tiled=True)]
    all_gather x1 -> x0, blocking collectives: 306 us -> none  [body(): lax.all_gather(gains.astype(jnp.bfloat16), ('dp', 'seq'), axis=2, tiled=T...]
    unnamed x16 -> x3, waiting for transfers between devices: 162 us -> 0.05 us
    dot_general x36 -> x24, matrix products: 159 us -> 40.4 us  [dot(): return lax.dot_general(a, b, (dims, ((), ())), preferred_element_type=f32)]
    ppermute x0 -> x47, waiting for transfers between devices: none -> 107 us  [the longest x24 91.9 us: pair_swap(): return lax.ppermute(x, ALL, PAIRS[axis, phase])]
    all_to_all x0 -> x7, blocking collectives: none -> 98.7 us  [seq_swap(): return lax.all_to_all(x, SEQ, 0, 0, tiled=True)]
    ppermute x0 -> x47, starting transfers between devices: none -> 75 us  [the longest x24 38.5 us: pair_swap(): return lax.ppermute(x, ALL, PAIRS[axis, phase])]
  transfers between devices with their start and end apart: 14 -> 53, of which waited for: 13 -> 33; matrix products, arithmetic and copies ran while one was open for 3% -> 13% of each run, Pallas kernels for 0% -> 10%
where the time goes in v1:
time: 574 us; the launch traced here: 565 us
  waiting for transfers between devices  163 us (28%)
  blocking collectives  98.7 us (17%)
  starting transfers between devices  87.9 us (15%)
  local copies, waits for them, and re-layouts  63.8 us (11%)
  Pallas kernels  60.3 us (11%)
  matrix products  40.4 us (7%)
  other arithmetic  33.9 us (6%)
  between operations  16.5 us (3%)
    all_to_all x7, blocking collectives, seq_swap(): return lax.all_to_all(x, SEQ, 0, 0, tiled=True)  98.7 us
    ppermute x24, waiting for transfers between devices, pair_swap(): return lax.ppermute(x, ALL, PAIRS[axis, phase])  91.9 us
    dot_general x24, matrix products, dot(): return lax.dot_general(a, b, (dims, ((), ())), preferred_element_type=f32)  40.4 us
    ppermute x24, starting transfers between devices, pair_swap(): return lax.ppermute(x, ALL, PAIRS[axis, phase])  38.5 us
    unnamed x218, local copies, waits for them, and re-layouts  36.4 us
    all_gather x1, waiting for transfers between devices, body(): layer_buffer = lax.all_gather(line, XY, axis=0, tiled=True)  27.1 us
    pallas_call x3, Pallas kernels, pack(): pl.pallas_call(kernel, out_shape=tuple((jax.ShapeDtypeStruct(shape, bf16)...  23.6 us
    ppermute x17, starting transfers between devices, other_core(): return lax.ppermute(x, 'c', [(0, 1), (1, 0)])  20.8 us
  transfers between devices with their start and end apart: 53, of which 33 were waited for; matrix products, arithmetic and copies ran while one was open for 13% of the time, Pallas kernels for 10%

profile of v1, /device:TPU:1, one launch (start us, length us, event | category | flops | bytes accessed | tf_op | source)
XLA Modules:
  0.0 564.5 jit_solution(912291289756796832)
XLA Ops:
  17.5 3.7 multiply_sine_fusion
  23.9 5.0 all-to-all-start
  29.0 3.6 collective-permute-start.3
  32.6 3.1 collective-permute-done.3
  35.7 5.7 %all-to-all-done = bf16[8,16,6272]{2,1,0:T(8,128)(2,1)S(1)} async-done(((bf16[8,16,6272]{2,1,0:T(8,128)(2,1)}), bf16[8,16,6272]{2,1,0:T(8,128)(2,1)S(1)}, u32[]{:S(2)}, u32[]{:S(2)}) %all-to-all-start) | async-done | bytes 1605664 | tf_op jit(solution)/shard_map/all_to_all | solution.py:266
  49.3 8.0 %collective-permute-done.5 = bf16[2,16,6144]{2,1,0:T(8,128)(2,1)S(1)} collective-permute-done((bf16[2,16,6144]{2,1,0:T(8,128)(2,1)S(1)}, bf16[2,16,6144]{2,1,0:T(8,128)(2,1)S(1)}, u32[]{:S(2)}, u32[]{:S(2)}) %collective-permute-start.5) | collective-permute-done | bytes 393248 | tf_op jit(solution)/shard_map/ppermute | solution.py:244
  60.3 12.1 %collective-permute-done.11 = bf16[16,16,2048]{2,1,0:T(8,128)(2,1)S(1)} collective-permute-done((bf16[16,16,2048]{2,1,0:T(8,128)(2,1)S(1)}, bf16[16,16,2048]{2,1,0:T(8,128)(2,1)S(1)}, u32[]{:S(2)}, u32[]{:S(2)}) %collective-permute-start.11) | collective-permute-done | bytes 1048608 | tf_op jit(solution)/shard_map/ppermute | solution.py:244
  80.2 20.1 %collective-permute-done.12.refs_3_ = bf16[32,16,2048]{2,1,0:T(8,128)(2,1)} collective-permute-done((bf16[32,16,2048]{2,1,0:T(8,128)(2,1)}, bf16[32,16,2048]{2,1,0:T(8,128)(2,1)}, u32[]{:S(2)}, u32[]{:S(2)}) %collective-permute-start.12) | collective-permute-done | bytes 2097184 | tf_op jit(solution)/shard_map/ppermute | solution.py:244
  100.3 4.8 collective-permute-done.14.refs_5_
  106.5 5.2 unpack.2
  118.2 3.3 collective-permute-start.15
  125.0 19.1 %all_to_all.50 = bf16[8,128,384]{1,2,0:T(8,128)(2,1)S(1)} all-to-all(bf16[8,128,384]{1,2,0:T(8,128)(2,1)S(1)} %bitcast.212), channel_id=1, replica_groups=mesh['zh'=2,'x'=4,'c'=2,'y'=4,'zl'=2] {'y','zl'}, dimensions={0} | all-to-all | bytes 1572864 | tf_op jit(solution)/shard_map/all_to_all | solution.py:213
  144.5 4.6 att_forward.2
  150.2 12.2 %all_to_all.51 = bf16[8,128,128]{1,2,0:T(8,128)(2,1)S(1)} all-to-all(bf16[8,128,128]{1,2,0:T(8,128)(2,1)S(1)} %copy.142), channel_id=1, replica_groups=mesh['zh'=2,'x'=4,'c'=2,'y'=4,'zl'=2] {'y','zl'}, dimensions={0} | all-to-all | bytes 524288 | tf_op jit(solution)/shard_map/all_to_all | solution.py:213
  169.1 7.2 %multiply_convert_fusion.1 = (bf16[256,2048]{1,0:T(8,128)(2,1)S(1)}, f32[256,2048]{1,0:T(8,128)}, f32[256,2048]{1,0:T(8,128)}) fusion(bf16[1024,2048]{1,0:T(8,128)(2,1)S(1)} %copy-done.14, bf16[128,1024]{1,0:T(8,128)(2,1)S(1)} %collective-permute-done.17, bf16[128,1024]{1,0:T(8,128)(2,1)S(1)} %multiply_convert_fusion.7), kind=kOutput, calls=%fused_computation.30 | convolution fusion | flops 1108869120 | bytes 9961472 | tf_op jit(solution)/shard_map/dot_general | solution.py:39
  180.7 27.1 %all-gather.2.cloned.1.call-done.refs_0_ = bf16[64,16,6144]{2,1,0:T(8,128)(2,1)} async-done(((bf16[4,16,6144]{2,1,0:T(8,128)(2,1)}), bf16[64,16,6144]{2,1,0:T(8,128)(2,1)}) %all-gather.2.cloned.1.call-update) | async-done | bytes 12582928 | tf_op jit(solution)/shard_map/all_gather | solution.py:554
  207.8 4.6 copy-done.2
  212.4 10.9 %unpack.3 = (bf16[1024,1536]{1,0:T(8,128)(2,1)S(1)}, bf16[512,1024]{1,0:T(8,128)(2,1)S(1)}, bf16[1024,2048]{1,0:T(8,128)(2,1)S(1)}, bf16[2048,1024]{1,0:T(8,128)(2,1)S(1)}) custom-call(s32[20,64]{1,0:T(8,128)S(1)} %stack.107.tab, bf16[64,16,6144]{2,1,0:T(8,128)(2,1)S(1)} %copy-done.2), custom_call_target="tpu_custom_call" | custom-call | tf_op jit(solution)/shard_map/unpack/pallas_call | solution.py:373
  235.6 14.9 %all_to_all.52 = bf16[8,128,384]{1,2,0:T(8,128)(2,1)} all-to-all(bf16[8,128,384]{1,2,0:T(8,128)(2,1)S(1)} %bitcast.214), channel_id=1, replica_groups=mesh['zh'=2,'x'=4,'c'=2,'y'=4,'zl'=2] {'y','zl'}, dimensions={0} | all-to-all | bytes 1572864 | tf_op jit(solution)/shard_map/all_to_all | solution.py:213
  251.9 4.6 att_forward.3
  260.0 9.2 %all_to_all.53 = bf16[8,128,128]{1,2,0:T(8,128)(2,1)S(1)} all-to-all(bf16[8,128,128]{1,2,0:T(8,128)(2,1)} %copy.147), channel_id=1, replica_groups=mesh['zh'=2,'x'=4,'c'=2,'y'=4,'zl'=2] {'y','zl'}, dimensions={0} | all-to-all | bytes 524288 | tf_op jit(solution)/shard_map/all_to_all | solution.py:213
  270.0 3.4 collective-permute-start.20
  276.8 5.6 multiply_convert_fusion
  295.0 7.5 %pack.3 = bf16[64,16,4096]{2,1,0:T(8,128)(2,1)S(1)} custom-call(s32[20,64]{1,0:T(8,128)S(1)} %stack.107.tab, bf16[1024,2048]{1,0:T(8,128)(2,1)S(1)} %convolution_convert_fusion.5.refs_0_, bf16[2048,1024]{1,0:T(8,128)(2,1)S(1)} %convolution_convert_fusion.4.refs_1_), custom_call_target="tpu_custom_call" | custom-call | tf_op jit(solution)/shard_map/pack/pallas_call | solution.py:409
  302.5 3.2 copy-done.1
  315.7 10.8 %all_to_all.54 = bf16[8,128,128]{1,2,0:T(8,128)(2,1)S(1)} all-to-all(bf16[8,128,128]{1,2,0:T(8,128)(2,1)S(1)} %bitcast.234), channel_id=1, replica_groups=mesh['zh'=2,'x'=4,'c'=2,'y'=4,'zl'=2] {'y','zl'}, dimensions={0} | all-to-all | bytes 524288 | tf_op jit(solution)/shard_map/all_to_all | solution.py:213
  327.8 5.7 %att_backward.2 = bf16[1024,384]{1,0:T(8,128)(2,1)S(1)} custom-call(bf16[1024,384]{1,0:T(8,128)(2,1)S(1)} %copy-done.11, bf16[1024,128]{1,0:T(8,128)(2,1)S(1)} %bitcast.208, f32[8,1024]{1,0:T(8,128)S(1)} %get-tuple-element.95.lse_ref, f32[1024,128]{1,0:T(8,128)S(1)} %pad_maximum_fusion.7.cos_ref, f32[1024,128]{1,0:T(8,128)S(1)} %pad_maximum_fusion.8.sin_ref, ...), custom_call_target="tpu_custom_call" | custom-call | tf_op jit(solution)/shard_map/att_backward/pallas_call | solution.py:159
  334.7 22.8 %all_to_all.55 = bf16[8,128,384]{1,2,0:T(8,128)(2,1)S(1)} all-to-all(bf16[8,128,384]{1,2,0:T(8,128)(2,1)} %copy.152), channel_id=1, replica_groups=mesh['zh'=2,'x'=4,'c'=2,'y'=4,'zl'=2] {'y','zl'}, dimensions={0} | all-to-all | bytes 1572864 | tf_op jit(solution)/shard_map/all_to_all | solution.py:213
  359.5 3.2 collective-permute-start.26
  374.8 10.9 %pack.4 = bf16[64,16,6144]{2,1,0:T(8,128)(2,1)S(1)} custom-call(s32[20,64]{1,0:T(8,128)S(1)} %stack.107.tab, bf16[1024,1536]{1,0:T(8,128)(2,1)S(1)} %convolution_convert_fusion.1.refs_0_, bf16[512,1024]{1,0:T(8,128)(2,1)S(1)} %convolution_convert_fusion.9.refs_1_, bf16[1024,2048]{1,0:T(8,128)(2,1)S(1)} %convolution_convert_fusion.3.refs_2_, ...), custom_call_target="tpu_custom_call" | custom-call | tf_op jit(solution)/shard_map/pack/pallas_call | solution.py:409
  385.8 4.6 copy-done
  398.9 9.7 %all_to_all.56 = bf16[8,128,128]{1,2,0:T(8,128)(2,1)S(1)} all-to-all(bf16[8,128,128]{1,2,0:T(8,128)(2,1)S(1)} %bitcast.236), channel_id=1, replica_groups=mesh['zh'=2,'x'=4,'c'=2,'y'=4,'zl'=2] {'y','zl'}, dimensions={0} | all-to-all | bytes 524288 | tf_op jit(solution)/shard_map/all_to_all | solution.py:213
  410.2 5.7 %att_backward.3 = bf16[1024,384]{1,0:T(8,128)(2,1)S(1)} custom-call(bf16[1024,384]{1,0:T(8,128)(2,1)S(1)} %copy-done.9, bf16[1024,128]{1,0:T(8,128)(2,1)S(1)} %bitcast.207, f32[8,1024]{1,0:T(8,128)S(1)} %get-tuple-element.97.lse_ref, f32[1024,128]{1,0:T(8,128)S(1)} %pad_maximum_fusion.7.cos_ref, f32[1024,128]{1,0:T(8,128)S(1)} %pad_maximum_fusion.8.sin_ref, ...), custom_call_target="tpu_custom_call" | custom-call | tf_op jit(solution)/shard_map/att_backward/pallas_call | solution.py:159
  417.1 4.2 all-to-all-start.8
  424.2 17.7 %all-to-all-done.8 = bf16[8,128,384]{1,2,0:T(8,128)(2,1)} async-done(((bf16[8,128,384]{1,2,0:T(8,128)(2,1)}), bf16[8,128,384]{1,2,0:T(8,128)(2,1)}, u32[]{:S(2)}, u32[]{:S(2)}) %all-to-all-start.8) | async-done | bytes 786464 | tf_op jit(solution)/shard_map/all_to_all | solution.py:213
  452.4 5.2 pack.5
  461.4 2.8 collective-permute-start.34
  464.2 15.8 %collective-permute-done.37 = bf16[32,16,640]{2,1,0:T(8,128)(2,1)S(1)} collective-permute-done((bf16[32,16,640]{2,1,0:T(8,128)(2,1)S(1)}, bf16[32,16,640]{2,1,0:T(8,128)(2,1)S(1)}, u32[]{:S(2)}, u32[]{:S(2)}) %collective-permute-start.37) | collective-permute-done | bytes 655392 | tf_op jit(solution)/shard_map/ppermute | solution.py:244
  483.3 4.1 collective-permute-done.38
  487.5 3.0 collective-permute-start.39
  490.9 2.8 collective-permute-done.39
  495.6 3.5 collective-permute-done.35
  500.7 3.5 collective-permute-done.33
  504.3 3.0 collective-permute-done.36
  508.2 3.5 all-to-all-start.9
  512.7 5.6 all-to-all-done.9
  531.2 6.2 %collective-permute-done.41 = bf16[1,16,6144]{2,1,0:T(8,128)(2,1)S(1)} collective-permute-done((bf16[1,16,6144]{2,1,0:T(8,128)(2,1)S(1)}, bf16[1,16,6144]{2,1,0:T(8,128)(2,1)S(1)}, u32[]{:S(2)}, u32[]{:S(2)}) %collective-permute-start.41) | collective-permute-done | bytes 196640 | tf_op jit(solution)/shard_map/ppermute | solution.py:244
  538.1 11.8 %collective-permute-start.44 = (bf16[8,7296]{1,0:T(8,128)(2,1)S(1)}, bf16[8,7296]{1,0:T(8,128)(2,1)S(1)}, u32[]{:S(2)}, u32[]{:S(2)}) collective-permute-start(bf16[8,7296]{1,0:T(8,128)(2,1)S(1)} %get-tuple-element.197), channel_id=1, source_target_pairs={{0,0},{2,2},{4,4},{6,6},{1,8},{3,10},{5,12},{7,14},{16,16},{18,18}... | collective-permute-start | bytes 350216 | tf_op jit(solution)/shard_map/ppermute | solution.py:456
  (520 shorter events, 173.2 us)
Async XLA Ops:
  7.2 9.9 %collective-permute-start.4 = (s32[1,4]{1,0:T(1,128)}, s32[1,4]{1,0:T(1,128)S(1)}, u32[]{:S(2)}, u32[]{:S(2)}) collective-permute-start(s32[1,4]{1,0:T(1,128)} %param.20), channel_id=1, source_target_pairs={{0,8},{8,0},{1,9},{9,1},{2,10},{10,2},{3,11},{11,3},{4,12},{12,4},... | collective-permute-start | bytes 56 | tf_op jit(solution)/shard_map/ppermute | solution.py:200
  9.6 12.9 %collective-permute-start.2 = (bf16[2,8,512]{2,1,0:T(8,128)(2,1)S(1)}, bf16[2,8,512]{2,1,0:T(8,128)(2,1)S(1)}, u32[]{:S(2)}, u32[]{:S(2)}) collective-permute-start(bf16[2,8,512]{2,1,0:T(8,128)(2,1)S(1)} %get-tuple-element.220), channel_id=1, source_target_pairs={{0,1},{1,0},{2,3},{3,2},{4,5},{5,4},{6,7},{7,6},{8,9},{9,8},{10,11... | collective-permute-start | bytes 49160 | tf_op jit(solution)/shard_map/ppermute | solution.py:462
  14.7 7.7 %collective-permute-start = (bf16[8,7296]{1,0:T(8,128)(2,1)S(1)}, bf16[8,7296]{1,0:T(8,128)(2,1)S(1)}, u32[]{:S(2)}, u32[]{:S(2)}) collective-permute-start(bf16[8,7296]{1,0:T(8,128)(2,1)S(1)} %get-tuple-element.203), channel_id=1, source_target_pairs={{0,0},{2,2},{4,4},{6,6},{8,1},{10,3},{12,5},{14,7},{16,16},{18,18}... | collective-permute-start | bytes 350216 | tf_op jit(solution)/shard_map/ppermute | solution.py:450
  16.7 5.8 %collective-permute-start.1 = (bf16[8,7296]{1,0:T(8,128)(2,1)S(1)}, bf16[8,7296]{1,0:T(8,128)(2,1)S(1)}, u32[]{:S(2)}, u32[]{:S(2)}) collective-permute-start(bf16[8,7296]{1,0:T(8,128)(2,1)S(1)} %get-tuple-element.204), channel_id=1, source_target_pairs={{0,8},{2,10},{4,12},{6,14},{8,9},{10,11},{12,13},{14,15},{16,24},{... | collective-permute-start | bytes 350216 | tf_op jit(solution)/shard_map/ppermute | solution.py:451
  23.9 17.5 %all-to-all-start = ((bf16[8,16,6272]{2,1,0:T(8,128)(2,1)}), bf16[8,16,6272]{2,1,0:T(8,128)(2,1)S(1)}, u32[]{:S(2)}, u32[]{:S(2)}) async-start(bf16[8,16,6272]{2,1,0:T(8,128)(2,1)} %broadcast_in_dim.22), calls=%async_computation | async-start | bytes 3211264 | tf_op jit(solution)/shard_map/all_to_all | solution.py:266
  28.9 178.9 %all-gather.2.cloned.1.call-start = ((), (), s32[]{:S(2)}) async-start(), calls=%async_computation.12 | async-start | bytes 13369344 | tf_op jit(solution)/shard_map/all_gather | solution.py:554
  29.0 6.7 %collective-permute-start.3 = (bf16[1,16,6144]{2,1,0:T(8,128)(2,1)S(1)}, bf16[1,16,6144]{2,1,0:T(8,128)(2,1)S(1)}, u32[]{:S(2)}, u32[]{:S(2)}) collective-permute-start(bf16[1,16,6144]{2,1,0:T(8,128)(2,1)S(1)} %maximum_bitcast_fusion), channel_id=1, source_target_pairs={{0,1},{1,0},{2,3},{3,2},{4,5},{5,4},{6,7},{7,6},{8,73},{9,72},{10,... | collective-permute-start | bytes 589832 | tf_op jit(solution)/shard_map/ppermute | solution.py:244
  41.6 15.7 %collective-permute-start.8 = (bf16[8,16,2048]{2,1,0:T(8,128)(2,1)S(1)}, bf16[8,16,2048]{2,1,0:T(8,128)(2,1)S(1)}, u32[]{:S(2)}, u32[]{:S(2)}) collective-permute-start(bf16[8,16,2048]{2,1,0:T(8,128)(2,1)S(1)} %get-tuple-element.183), channel_id=1, source_target_pairs={{0,1},{1,0},{2,3},{3,2},{4,5},{5,4},{6,7},{7,6},{8,73},{9,72},{10,... | collective-permute-start | bytes 1572872 | tf_op jit(solution)/shard_map/ppermute | solution.py:244
  44.1 13.2 %collective-permute-start.7 = (bf16[8,16,2048]{2,1,0:T(8,128)(2,1)S(1)}, bf16[8,16,2048]{2,1,0:T(8,128)(2,1)S(1)}, u32[]{:S(2)}, u32[]{:S(2)}) collective-permute-start(bf16[8,16,2048]{2,1,0:T(8,128)(2,1)S(1)} %get-tuple-element.184), channel_id=1, source_target_pairs={{0,2},{1,3},{2,0},{3,1},{4,6},{5,7},{6,4},{7,5},{8,14},{9,15},{10,... | collective-permute-start | bytes 1572872 | tf_op jit(solution)/shard_map/ppermute | solution.py:244
  46.9 10.4 %collective-permute-start.6 = (bf16[8,16,2176]{2,1,0:T(8,128)(2,1)S(1)}, bf16[8,16,2176]{2,1,0:T(8,128)(2,1)S(1)}, u32[]{:S(2)}, u32[]{:S(2)}) collective-permute-start(bf16[8,16,2176]{2,1,0:T(8,128)(2,1)S(1)} %slice.334), channel_id=1, source_target_pairs={{0,16},{1,17},{2,18},{3,19},{4,20},{5,21},{6,22},{7,23},{8,56},{9,... | collective-permute-start | bytes 1671176 | tf_op jit(solution)/shard_map/ppermute | solution.py:244
  48.3 9.0 %collective-permute-start.5 = (bf16[2,16,6144]{2,1,0:T(8,128)(2,1)S(1)}, bf16[2,16,6144]{2,1,0:T(8,128)(2,1)S(1)}, u32[]{:S(2)}, u32[]{:S(2)}) collective-permute-start(bf16[2,16,6144]{2,1,0:T(8,128)(2,1)S(1)} %constant_dynamic-update-slice_fusion.3), channel_id=1, source_target_pairs={{0,65},{1,64},{2,67},{3,66},{4,69},{5,68},{6,71},{7,70},{8,9},{9,8... | collective-permute-start | bytes 1179656 | tf_op jit(solution)/shard_map/ppermute | solution.py:244
  57.4 14.9 %collective-permute-start.11 = (bf16[16,16,2048]{2,1,0:T(8,128)(2,1)S(1)}, bf16[16,16,2048]{2,1,0:T(8,128)(2,1)S(1)}, u32[]{:S(2)}, u32[]{:S(2)}) collective-permute-start(bf16[16,16,2048]{2,1,0:T(8,128)(2,1)S(1)} %pad_maximum_fusion.4), channel_id=1, source_target_pairs={{0,1},{1,0},{2,3},{3,2},{4,5},{5,4},{6,7},{7,6},{8,73},{9,72},{10,... | collective-permute-start | bytes 3145736 | tf_op jit(solution)/shard_map/ppermute | solution.py:244
  58.8 16.6 %collective-permute-start.9 = (bf16[16,16,2176]{2,1,0:T(8,128)(2,1)S(1)}, bf16[16,16,2176]{2,1,0:T(8,128)(2,1)S(1)}, u32[]{:S(2)}, u32[]{:S(2)}) collective-permute-start(bf16[16,16,2176]{2,1,0:T(8,128)(2,1)S(1)} %pad_maximum_fusion.3), channel_id=1, source_target_pairs={{0,2},{1,3},{2,0},{3,1},{4,6},{5,7},{6,4},{7,5},{8,14},{9,15},{10,... | collective-permute-start | bytes 3342344 | tf_op jit(solution)/shard_map/ppermute | solution.py:244
  59.0 17.7 %collective-permute-start.13 = (bf16[16,16,2048]{2,1,0:T(8,128)(2,1)S(1)}, bf16[16,16,2048]{2,1,0:T(8,128)(2,1)S(1)}, u32[]{:S(2)}, u32[]{:S(2)}) collective-permute-start(bf16[16,16,2048]{2,1,0:T(8,128)(2,1)S(1)} %pad_maximum_fusion.5), channel_id=1, source_target_pairs={{0,16},{1,17},{2,18},{3,19},{4,20},{5,21},{6,22},{7,23},{8,56},{9,... | collective-permute-start | bytes 3145736 | tf_op jit(solution)/shard_map/ppermute | solution.py:244
  73.9 26.4 %collective-permute-start.12 = (bf16[32,16,2048]{2,1,0:T(8,128)(2,1)}, bf16[32,16,2048]{2,1,0:T(8,128)(2,1)}, u32[]{:S(2)}, u32[]{:S(2)}) collective-permute-start(bf16[32,16,2048]{2,1,0:T(8,128)(2,1)} %pad_maximum_fusion.1.refs_2_), channel_id=1, source_target_pairs={{0,16},{1,17},{2,18},{3,19},{4,20},{5,21},{6,22},{7,23},{8,56},{9,... | collective-permute-start | bytes 6291464 | tf_op jit(solution)/shard_map/ppermute | solution.py:244
  75.7 29.4 %collective-permute-start.10 = (bf16[32,16,2176]{2,1,0:T(8,128)(2,1)S(1)}, bf16[32,16,2176]{2,1,0:T(8,128)(2,1)}, u32[]{:S(2)}, u32[]{:S(2)}) collective-permute-start(bf16[32,16,2176]{2,1,0:T(8,128)(2,1)S(1)} %pad_maximum_fusion.refs_0_), channel_id=1, source_target_pairs={{0,1},{1,0},{2,3},{3,2},{4,5},{5,4},{6,7},{7,6},{8,73},{9,72},{10,... | collective-permute-start | bytes 6684680 | tf_op jit(solution)/shard_map/ppermute | solution.py:244
  78.2 26.9 %collective-permute-start.14 = (bf16[32,16,2048]{2,1,0:T(8,128)(2,1)}, bf16[32,16,2048]{2,1,0:T(8,128)(2,1)}, u32[]{:S(2)}, u32[]{:S(2)}) collective-permute-start(bf16[32,16,2048]{2,1,0:T(8,128)(2,1)} %pad_maximum_fusion.2.refs_4_), channel_id=1, source_target_pairs={{0,2},{1,3},{2,0},{3,1},{4,6},{5,7},{6,4},{7,5},{8,14},{9,15},{10,... | collective-permute-start | bytes 6291464 | tf_op jit(solution)/shard_map/ppermute | solution.py:244
  105.1 413.3 %reduce-scatter.5.cloned.1.call-start = ((), (), s32[]{:S(2)}) async-start(), calls=%async_computation.14 | async-start | bytes 8912896 | tf_op jit(solution)/shard_map/reduce_scatter | solution.py:429
  118.2 4.5 collective-permute-start.15
  163.5 3.3 collective-permute-start.16
  167.3 1.8 collective-permute-start.17
  177.7 1.6 collective-permute-start.18
  180.2 48.0 %collective-permute-start.19 = (bf16[128,1024]{1,0:T(8,128)(2,1)S(1)}, bf16[128,1024]{1,0:T(8,128)(2,1)S(1)}, u32[]{:S(2)}, u32[]{:S(2)}) collective-permute-start(bf16[128,1024]{1,0:T(8,128)(2,1)S(1)} %multiply_convert_fusion.6), channel_id=1, source_target_pairs={{0,8},{8,0},{1,9},{9,1},{2,10},{10,2},{3,11},{11,3},{4,12},{12,4},... | collective-permute-start | bytes 786440 | tf_op jit(solution)/shard_map/ppermute | solution.py:200
  270.0 4.5 collective-permute-start.20
  283.7 1.6 collective-permute-start.22
  291.6 14.2 %collective-permute-start.24 = (bf16[128,1024]{1,0:T(8,128)(2,1)S(1)}, bf16[128,1024]{1,0:T(8,128)(2,1)S(1)}, u32[]{:S(2)}, u32[]{:S(2)}) collective-permute-start(bf16[128,1024]{1,0:T(8,128)(2,1)S(1)} %slice.612), channel_id=1, source_target_pairs={{0,8},{8,0},{1,9},{9,1},{2,10},{10,2},{3,11},{11,3},{4,12},{12,4},... | collective-permute-start | bytes 786440 | tf_op jit(solution)/shard_map/ppermute | solution.py:200
  306.6 213.4 %reduce-scatter.3.cloned.1.call-start = ((), (), s32[]{:S(2)}) async-start(), calls=%async_computation.13 | async-start | bytes 13369344 | tf_op jit(solution)/shard_map/reduce_scatter | solution.py:429
  359.5 4.3 collective-permute-start.26
  371.8 18.6 %collective-permute-start.28 = (bf16[128,1024]{1,0:T(8,128)(2,1)S(1)}, bf16[128,1024]{1,0:T(8,128)(2,1)S(1)}, u32[]{:S(2)}, u32[]{:S(2)}) collective-permute-start(bf16[128,1024]{1,0:T(8,128)(2,1)S(1)} %slice.610), channel_id=1, source_target_pairs={{0,8},{8,0},{1,9},{9,1},{2,10},{10,2},{3,11},{11,3},{4,12},{12,4},... | collective-permute-start | bytes 786440 | tf_op jit(solution)/shard_map/ppermute | solution.py:200
  417.1 24.8 %all-to-all-start.8 = ((bf16[8,128,384]{1,2,0:T(8,128)(2,1)}), bf16[8,128,384]{1,2,0:T(8,128)(2,1)}, u32[]{:S(2)}, u32[]{:S(2)}) async-start(bf16[8,128,384]{1,2,0:T(8,128)(2,1)} %copy.157), calls=%async_computation.8 | async-start | bytes 1572864 | tf_op jit(solution)/shard_map/all_to_all | solution.py:213
  445.1 3.5 collective-permute-start.30
  457.7 22.3 %collective-permute-start.37 = (bf16[32,16,640]{2,1,0:T(8,128)(2,1)S(1)}, bf16[32,16,640]{2,1,0:T(8,128)(2,1)S(1)}, u32[]{:S(2)}, u32[]{:S(2)}) collective-permute-start(bf16[32,16,640]{2,1,0:T(8,128)(2,1)S(1)} %get-tuple-element.103), channel_id=1, source_target_pairs={{0,2},{1,3},{2,0},{3,1},{4,6},{5,7},{6,4},{7,5},{8,14},{9,15},{10,... | collective-permute-start | bytes 1966088 | tf_op jit(solution)/shard_map/ppermute | solution.py:244
  458.7 22.8 %collective-permute-start.31 = (bf16[32,16,768]{2,1,0:T(8,128)(2,1)S(1)}, bf16[32,16,768]{2,1,0:T(8,128)(2,1)S(1)}, u32[]{:S(2)}, u32[]{:S(2)}) collective-permute-start(bf16[32,16,768]{2,1,0:T(8,128)(2,1)S(1)} %get-tuple-element.99), channel_id=1, source_target_pairs={{0,1},{1,0},{2,3},{3,2},{4,5},{5,4},{6,7},{7,6},{8,73},{9,72},{10,... | collective-permute-start | bytes 2359304 | tf_op jit(solution)/shard_map/ppermute | solution.py:244
  461.4 29.2 %collective-permute-start.34 = (bf16[32,16,768]{2,1,0:T(8,128)(2,1)S(1)}, bf16[32,16,768]{2,1,0:T(8,128)(2,1)S(1)}, u32[]{:S(2)}, u32[]{:S(2)}) collective-permute-start(bf16[32,16,768]{2,1,0:T(8,128)(2,1)S(1)} %get-tuple-element.101), channel_id=1, source_target_pairs={{0,16},{1,17},{2,18},{3,19},{4,20},{5,21},{6,22},{7,23},{8,56},{9,... | collective-permute-start | bytes 2359304 | tf_op jit(solution)/shard_map/ppermute | solution.py:244
  480.2 7.2 %collective-permute-start.38 = (bf16[16,16,640]{2,1,0:T(8,128)(2,1)S(1)}, bf16[16,16,640]{2,1,0:T(8,128)(2,1)S(1)}, u32[]{:S(2)}, u32[]{:S(2)}) collective-permute-start(bf16[16,16,640]{2,1,0:T(8,128)(2,1)S(1)} %slice.458), channel_id=1, source_target_pairs={{0,16},{1,17},{2,18},{3,19},{4,20},{5,21},{6,22},{7,23},{8,56},{9,... | collective-permute-start | bytes 983048 | tf_op jit(solution)/shard_map/ppermute | solution.py:244
  481.7 12.1 %collective-permute-start.32 = (bf16[16,16,768]{2,1,0:T(8,128)(2,1)S(1)}, bf16[16,16,768]{2,1,0:T(8,128)(2,1)S(1)}, u32[]{:S(2)}, u32[]{:S(2)}) collective-permute-start(bf16[16,16,768]{2,1,0:T(8,128)(2,1)S(1)} %slice.448), channel_id=1, source_target_pairs={{0,2},{1,3},{2,0},{3,1},{4,6},{5,7},{6,4},{7,5},{8,14},{9,15},{10,... | collective-permute-start | bytes 1179656 | tf_op jit(solution)/shard_map/ppermute | solution.py:244
  487.5 6.2 %collective-permute-start.39 = (bf16[8,16,640]{2,1,0:T(8,128)(2,1)S(1)}, bf16[8,16,640]{2,1,0:T(8,128)(2,1)S(1)}, u32[]{:S(2)}, u32[]{:S(2)}) collective-permute-start(bf16[8,16,640]{2,1,0:T(8,128)(2,1)S(1)} %slice.460), channel_id=1, source_target_pairs={{0,1},{1,0},{2,3},{3,2},{4,5},{5,4},{6,7},{7,6},{8,73},{9,72},{10,... | collective-permute-start | bytes 491528 | tf_op jit(solution)/shard_map/ppermute | solution.py:244
  490.8 8.3 %collective-permute-start.35 = (bf16[16,16,768]{2,1,0:T(8,128)(2,1)S(1)}, bf16[16,16,768]{2,1,0:T(8,128)(2,1)S(1)}, u32[]{:S(2)}, u32[]{:S(2)}) collective-permute-start(bf16[16,16,768]{2,1,0:T(8,128)(2,1)S(1)} %slice.453), channel_id=1, source_target_pairs={{0,1},{1,0},{2,3},{3,2},{4,5},{5,4},{6,7},{7,6},{8,73},{9,72},{10,... | collective-permute-start | bytes 1179656 | tf_op jit(solution)/shard_map/ppermute | solution.py:244
  493.9 10.3 %collective-permute-start.33 = (bf16[8,16,768]{2,1,0:T(8,128)(2,1)S(1)}, bf16[8,16,768]{2,1,0:T(8,128)(2,1)S(1)}, u32[]{:S(2)}, u32[]{:S(2)}) collective-permute-start(bf16[8,16,768]{2,1,0:T(8,128)(2,1)S(1)} %slice.450), channel_id=1, source_target_pairs={{0,16},{1,17},{2,18},{3,19},{4,20},{5,21},{6,22},{7,23},{8,56},{9,... | collective-permute-start | bytes 589832 | tf_op jit(solution)/shard_map/ppermute | solution.py:244
  499.3 8.0 %collective-permute-start.36 = (bf16[8,16,768]{2,1,0:T(8,128)(2,1)S(1)}, bf16[8,16,768]{2,1,0:T(8,128)(2,1)S(1)}, u32[]{:S(2)}, u32[]{:S(2)}) collective-permute-start(bf16[8,16,768]{2,1,0:T(8,128)(2,1)S(1)} %slice.455), channel_id=1, source_target_pairs={{0,2},{1,3},{2,0},{3,1},{4,6},{5,7},{6,4},{7,5},{8,14},{9,15},{10,... | collective-permute-start | bytes 589832 | tf_op jit(solution)/shard_map/ppermute | solution.py:244
  508.2 10.1 %all-to-all-start.9 = ((bf16[8,16,2176]{2,1,0:T(8,128)(2,1)}), bf16[8,16,2176]{2,1,0:T(8,128)(2,1)S(1)}, u32[]{:S(2)}, u32[]{:S(2)}) async-start(bf16[8,16,2176]{2,1,0:T(8,128)(2,1)} %maximum_maximum_fusion), calls=%async_computation.9 | async-start | bytes 1114112 | tf_op jit(solution)/shard_map/all_to_all | solution.py:266
  519.5 5.3 collective-permute-start.42
  521.2 7.9 %collective-permute-start.40 = (bf16[2,16,6144]{2,1,0:T(8,128)(2,1)S(1)}, bf16[2,16,6144]{2,1,0:T(8,128)(2,1)S(1)}, u32[]{:S(2)}, u32[]{:S(2)}) collective-permute-start(bf16[2,16,6144]{2,1,0:T(8,128)(2,1)S(1)} %bitcast.241), channel_id=1, source_target_pairs={{0,65},{1,64},{2,67},{3,66},{4,69},{5,68},{6,71},{7,70},{8,9},{9,8... | collective-permute-start | bytes 1179656 | tf_op jit(solution)/shard_map/ppermute | solution.py:244
  524.9 6.3 %collective-permute-start.43 = (bf16[1,16,4096]{2,1,0:T(8,128)(2,1)S(1)}, bf16[1,16,4096]{2,1,0:T(8,128)(2,1)S(1)}, u32[]{:S(2)}, u32[]{:S(2)}) collective-permute-start(bf16[1,16,4096]{2,1,0:T(8,128)(2,1)S(1)} %slice.475), channel_id=1, source_target_pairs={{0,1},{1,0},{2,3},{3,2},{4,5},{5,4},{6,7},{7,6},{8,73},{9,72},{10,... | collective-permute-start | bytes 393224 | tf_op jit(solution)/shard_map/ppermute | solution.py:244
  529.2 8.3 %collective-permute-start.41 = (bf16[1,16,6144]{2,1,0:T(8,128)(2,1)S(1)}, bf16[1,16,6144]{2,1,0:T(8,128)(2,1)S(1)}, u32[]{:S(2)}, u32[]{:S(2)}) collective-permute-start(bf16[1,16,6144]{2,1,0:T(8,128)(2,1)S(1)} %slice.469), channel_id=1, source_target_pairs={{0,1},{1,0},{2,3},{3,2},{4,5},{5,4},{6,7},{7,6},{8,73},{9,72},{10,... | collective-permute-start | bytes 589832 | tf_op jit(solution)/shard_map/ppermute | solution.py:244
  538.0 13.1 %collective-permute-start.46 = (bf16[2,8,512]{2,1,0:T(8,128)(2,1)S(1)}, bf16[2,8,512]{2,1,0:T(8,128)(2,1)S(1)}, u32[]{:S(2)}, u32[]{:S(2)}) collective-permute-start(bf16[2,8,512]{2,1,0:T(8,128)(2,1)S(1)} %get-tuple-element.217), channel_id=1, source_target_pairs={{0,1},{1,0},{2,3},{3,2},{4,5},{5,4},{6,7},{7,6},{8,9},{9,8},{10,11... | collective-permute-start | bytes 49160 | tf_op jit(solution)/shard_map/ppermute | solution.py:462
  538.1 14.3 %collective-permute-start.44 = (bf16[8,7296]{1,0:T(8,128)(2,1)S(1)}, bf16[8,7296]{1,0:T(8,128)(2,1)S(1)}, u32[]{:S(2)}, u32[]{:S(2)}) collective-permute-start(bf16[8,7296]{1,0:T(8,128)(2,1)S(1)} %get-tuple-element.197), channel_id=1, source_target_pairs={{0,0},{2,2},{4,4},{6,6},{1,8},{3,10},{5,12},{7,14},{16,16},{18,18}... | collective-permute-start | bytes 350216 | tf_op jit(solution)/shard_map/ppermute | solution.py:456
  549.9 3.7 collective-permute-start.45
  (109 other events, 641.4 us)
Sparse Core Ops, SparseCore 0:
  105.2 102.5 all-gather.1
  306.7 88.9 reduce-scatter.4
  399.2 108.6 reduce-scatter.2
